TPU v7x, 32 devices: a whole 2x2x4 slice. The times are simulated.
32 devices in a mesh: groups: 2 (over y), col: 4 (over z), sub: 4 (over x, core).
Axes of the slice: x: 2, y: 2, z: 4, core: 2. Of those that a mesh axis runs over, the one named last changes fastest.
Arguments:
- gcm_state: float32 [2, 72, 32, 512], P(None, None, ('groups', 'col'), 'sub'), parts along dimension 2, may hold values from -6 to 6
- crm_state: bfloat16 [2, 58, 32, 32, 512], P(None, None, None, ('groups', 'col'), 'sub'), parts along dimension 3, may hold values from -6 to 6
- active: int32 [32, 512], P(('groups', 'col'), 'sub'), parts along dimension 0, may hold values from 0 to 1, as said below
- wind_x: float32 [72], replicated, may hold values from 0.5 to 1.5
- wind_y: float32 [72], replicated, may hold values from -1.5 to -0.5
- courant: float32 [58], replicated, may hold values from 0.05 to 0.45
- relax: float32 [2, 58], replicated, may hold values from 0.05 to 0.4
- sat: float32 [58], replicated, may hold values from -4 to 4
- cond_rate: float32 [58], replicated, may hold values from 0.05 to 0.5
Outputs:
- gcm_new: float32 [2, 72, 32, 512], P(None, None, ('groups', 'col'), 'sub'), parts along dimension 2
- crm_new: bfloat16 [2, 58, 32, 32, 512], P(None, None, None, ('groups', 'col'), 'sub'), parts along dimension 3
There are 2 independent parts, one for each index of `groups`. A program takes and returns all parts, laid end to end along the dimension named above; an argument that names none is the same for every part. Nothing has to cross between parts.
Inputs may be any that keep to these rules, and one draw needn't show every extreme that they name: `active`: exactly 2048 entries are 1, and every column of at least one device's block of 4 x 128 columns is 1.
All inputs are finite; a program needn't handle non-finite values.
Results may differ from a plain program's by a relative error of at most 0.001.
The roundings to bfloat16 on the way count: a program that leaves them out, or rounds other values in their place, can miss the bound.
Values may be sent and summed in bfloat16 or wider, within the bound.
No kernel may reach another device: no remote copies, remote signals or barrier semaphores. Data moves between devices by JAX's collectives and lax.ppermute only.
A program may use at most 64 MiB of HBM per device.

v0:
```python
import jax
import jax.numpy as jnp
import numpy as np
from jax import lax
from jax.sharding import PartitionSpec as P

SUBSTEPS = 24


HIGH = lax.Precision.HIGHEST
DT_DYN = 0.05
DT_CLOUD = 0.5
KAPPA = 0.15


def extended(cells, sides, width):
    for axis, dim in sides:
        count = lax.axis_size(axis)
        head = lax.slice_in_dim(cells, 0, width, axis=dim)
        tail = lax.slice_in_dim(cells, cells.shape[dim] - width, cells.shape[dim], axis=dim)
        cells = jnp.concatenate(
            [
                lax.ppermute(tail, axis, [(i, (i + 1) % count) for i in range(count)]),
                cells,
                lax.ppermute(head, axis, [((i + 1) % count, i) for i in range(count)]),
            ],
            axis=dim,
        )
    return cells


def gll_derivative():
    nodes = np.array([-1.0, -1.0 / np.sqrt(5.0), 1.0 / np.sqrt(5.0), 1.0])
    weights = np.array(
        [1.0 / np.prod([nodes[j] - nodes[k] for k in range(4) if k != j]) for j in range(4)]
    )
    deriv = np.zeros((4, 4))
    for i in range(4):
        for j in range(4):
            if i != j:
                deriv[i, j] = weights[j] / weights[i] / (nodes[i] - nodes[j])
        deriv[i, i] = -deriv[i].sum()
    return 2.0 * deriv


def hat_matrix(count_to, count_from):
    dest = (jnp.arange(count_to, dtype=jnp.float32) + 0.5) / count_to
    source = (jnp.arange(count_from, dtype=jnp.float32) + 0.5) / count_from
    hat = jnp.maximum(0.0, 1.0 - jnp.abs(dest[:, None] - source[None, :]) * count_from)
    return hat / jnp.sum(hat, axis=1, keepdims=True)


def cloud_model(states, profile, courant, relax, sat, cond_rate):
    slots = states.shape[1]
    fields = relax.shape[0]
    levels = courant.shape[0]
    columns = states.shape[0] // (fields * levels)
    state = states.astype(jnp.float32).reshape(fields, levels, columns, slots)
    prof = profile.astype(jnp.float32).reshape(fields, -1, slots)
    target = jnp.einsum("kl,fls->fks", hat_matrix(levels, prof.shape[1]), prof, precision=HIGH)
    start = state

    def substep(index, current):
        upwind = current - jnp.roll(current, 1, axis=2)
        above = jnp.concatenate([current[:, 1:], current[:, -1:]], axis=1)
        below = jnp.concatenate([current[:, :1], current[:, :-1]], axis=1)
        change = (
            -courant[None, :, None, None] * upwind
            + KAPPA * (above + below - 2.0 * current)
            - DT_CLOUD * relax[:, :, None, None] * (current - target[:, :, None, :])
        )
        condense = DT_CLOUD * cond_rate[:, None, None] * jnp.tanh(current[1] - sat[:, None, None])
        return current + change + jnp.stack([condense, -condense])

    state = lax.fori_loop(0, SUBSTEPS, substep, state)
    mean_change = jnp.mean(state - start, axis=2).astype(jnp.bfloat16)
    return (state.astype(jnp.bfloat16).reshape(-1, slots), mean_change.reshape(-1, slots))


def send_out(state_part, prof_part):
    return (
        lax.all_to_all(state_part, ("col", "sub"), split_axis=1, concat_axis=1, tiled=True),
        lax.all_to_all(prof_part, ("col", "sub"), split_axis=1, concat_axis=1, tiled=True),
    )


def send_back(state_part, change_part):
    return (
        lax.all_to_all(state_part, ("col", "sub"), split_axis=1, concat_axis=1, tiled=True),
        lax.all_to_all(change_part, ("col", "sub"), split_axis=1, concat_axis=1, tiled=True),
    )


def advect(gcm_state, wind_x, wind_y):
    fields, levels, rows_x, rows_y = gcm_state.shape
    deriv = gll_derivative()
    step_x = jnp.asarray(np.kron(np.eye(rows_x // 4), deriv), jnp.float32)
    step_y = jnp.asarray(np.kron(np.eye(rows_y // 4), deriv), jnp.float32)
    along_x = jnp.einsum("ab,flbc->flac", step_x, gcm_state, precision=HIGH)
    along_y = jnp.einsum("flab,cb->flac", gcm_state, step_y, precision=HIGH)
    tendency = -(wind_x[None, :, None, None] * along_x + wind_y[None, :, None, None] * along_y)
    padded = extended(tendency, (("col", 2), ("sub", 3)), 1)
    node_x = (jnp.arange(rows_x) % 4)[:, None]
    centre = padded[:, :, 1:-1, :]
    half_x = jnp.where(
        node_x == 0,
        0.5 * (centre + padded[:, :, :-2, :]),
        jnp.where(node_x == 3, 0.5 * (centre + padded[:, :, 2:, :]), centre),
    )
    node_y = jnp.arange(rows_y) % 4
    middle = half_x[..., 1:-1]
    shared = jnp.where(
        node_y == 0,
        0.5 * (middle + half_x[..., :-2]),
        jnp.where(node_y == 3, 0.5 * (middle + half_x[..., 2:]), middle),
    )
    return gcm_state + DT_DYN * shared


def body(gcm_state, crm_state, active, wind_x, wind_y, courant, relax, sat, cond_rate):
    fields, levels, rows_x, rows_y = gcm_state.shape
    cloud_levels = courant.shape[0]
    columns_dev = rows_x * rows_y
    flat_active = active.reshape(columns_dev)
    profiles = gcm_state.reshape(fields * levels, columns_dev).astype(jnp.bfloat16)
    states = crm_state.reshape(-1, columns_dev)
    devices = lax.axis_size(("col", "sub"))
    peer_cap = columns_dev // devices
    total_slots = devices * peer_cap
    dense_slots = columns_dev // 4
    position_me = lax.axis_index(("col", "sub"))
    local_rank = jnp.cumsum(flat_active) - flat_active
    counts = lax.all_gather(jnp.sum(flat_active, keepdims=True), ("col", "sub"), axis=0, tiled=True)
    offsets = jnp.cumsum(counts) - counts
    own_offset = jnp.take(offsets, position_me)
    global_rank = own_offset + local_rank
    slot_of = jnp.where(
        flat_active > 0, global_rank % devices * peer_cap + local_rank // devices, total_slots
    )
    source = (
        jnp.zeros((total_slots,), jnp.int32)
        .at[slot_of]
        .set(jnp.arange(columns_dev, dtype=jnp.int32), mode="drop")
    )
    sent_state = jnp.take(states, source, axis=1).reshape(-1, devices, peer_cap)
    sent_prof = jnp.take(profiles, source, axis=1).reshape(-1, devices, peer_cap)
    got_state, got_prof = send_out(sent_state, sent_prof)
    dynamic = advect(gcm_state, wind_x, wind_y)
    flat_state = got_state.reshape(-1, total_slots)
    flat_prof = got_prof.reshape(-1, total_slots)
    first_rank = offsets + (position_me - offsets) % devices
    live = jnp.maximum(0, (offsets + counts - first_rank + devices - 1) // devices)
    within = jnp.arange(peer_cap, dtype=jnp.int32)
    dense_index = jnp.where(
        within[None, :] < live[:, None],
        first_rank[:, None] // devices + within[None, :],
        dense_slots,
    ).reshape(-1)
    pick = (
        jnp.zeros((dense_slots,), jnp.int32)
        .at[dense_index]
        .set(jnp.arange(total_slots, dtype=jnp.int32), mode="drop")
    )
    new_state, mean_change = cloud_model(
        jnp.take(flat_state, pick, axis=1),
        jnp.take(flat_prof, pick, axis=1),
        courant,
        relax,
        sat,
        cond_rate,
    )
    clipped = jnp.minimum(dense_index, dense_slots - 1)
    reply_state = jnp.take(new_state, clipped, axis=1)
    reply_change = jnp.take(mean_change, clipped, axis=1)
    back_state, back_change = send_back(
        reply_state.reshape(-1, devices, peer_cap), reply_change.reshape(-1, devices, peer_cap)
    )
    lookup = jnp.minimum(slot_of, total_slots - 1)
    mine_state = jnp.take(back_state.reshape(-1, total_slots), lookup, axis=1)
    mine_change = jnp.take(back_change.reshape(-1, total_slots), lookup, axis=1)
    keep = flat_active[None, :] > 0
    crm_new = jnp.where(keep, mine_state, states).reshape(crm_state.shape)
    feedback = jnp.einsum(
        "lk,fkc->flc",
        hat_matrix(levels, cloud_levels),
        mine_change.astype(jnp.float32).reshape(fields, cloud_levels, columns_dev),
        precision=HIGH,
    )
    flat_dynamic = dynamic.reshape(fields, levels, columns_dev)
    gcm_new = jnp.where(keep[None], flat_dynamic + feedback, flat_dynamic).reshape(gcm_state.shape)
    return (gcm_new, crm_new)


def solution(mesh):
    placed = (
        P(None, None, ("groups", "col"), "sub"),
        P(None, None, None, ("groups", "col"), "sub"),
        P(("groups", "col"), "sub"),
        P(),
        P(),
        P(),
        P(),
        P(),
        P(),
    )
    return jax.shard_map(
        body,
        mesh=mesh,
        in_specs=placed,
        out_specs=(
            P(None, None, ("groups", "col"), "sub"),
            P(None, None, None, ("groups", "col"), "sub"),
        ),
        check_vma=False,
    )
```

profile of v0, /device:TPU:13, one launch (start us, length us, event | category | flops | bytes accessed | tf_op | source)
XLA Modules:
  0.0 366.8 jit_solution(3026423599837454233)
XLA Ops:
  5.6 8.7 %all-reduce = s32[16]{0:T(128)S(1)} all-reduce(s32[16]{0:T(128)S(1)} %dynamic-update-slice.1), channel_id=1, replica_groups=mesh['groups'=2,'col'=4,'sub'=4] {'col','sub'}, use_global_device_ids=true, to_apply=%add | all-reduce | flops 16 | bytes 128
  16.9 2.4 scatter_custom_fusion.1
  23.4 7.6 %all-to-all-start.1 = ((bf16[144,16,32]{0,2,1:T(8,128)(2,1)}), bf16[144,16,32]{0,2,1:T(8,128)(2,1)S(1)}, u32[]{:S(2)}, u32[]{:S(2)}) async-start(bf16[144,16,32]{0,2,1:T(8,128)(2,1)} %broadcast_select_fusion.2), calls=%async_computation.1 | async-start | bytes 524288 | tf_op jit(solution)/shard_map/all_to_all | solution.py:83
  31.1 4.6 %copy.104 = bf16[464,8,4,128]{3,1,2,0:T(8,128)(2,1)} copy(bf16[464,8,4,128]{3,2,1,0:T(4,128)(2,1)} %bitcast.126) | data formatting | bytes 7602176
  35.7 6.1 %copy.77 = bf16[3712,512]{0,1:T(8,128)(2,1)} copy(bf16[3712,512]{1,0:T(8,128)(2,1)} %bitcast.121) | data formatting | bytes 7602176 | tf_op jit(solution)/shard_map/reshape | solution.py:126
  41.8 10.6 %gather_fusion.6 = bf16[512,3712]{1,0:T(8,128)(2,1)} fusion(bf16[3712,512]{0,1:T(8,128)(2,1)} %copy.77, s32[1024]{0:T(1024)S(1)} %pad_clamp_fusion.4), kind=kCustom, calls=%fused_computation.clone | custom fusion | bytes 7604224 | tf_op jit(solution)/shard_map/jit(_take)/gather | solution.py:145
  52.4 4.4 %broadcast_select_fusion = bf16[512,3712]{1,0:T(8,128)(2,1)} fusion(bf16[512,3712]{1,0:T(8,128)(2,1)} %gather_fusion.6, pred[512]{0:T(512)(128)(4,1)S(1)} %compare_and_fusion.1), kind=kLoop, calls=%fused_computation.24 | loop fusion | flops 1900544 | bytes 7602688 | tf_op jit(solution)/shard_map/jit(_take)/select_n | solution.py:145
  56.8 6.2 %all-to-all-start = ((bf16[3712,16,32]{0,2,1:T(8,128)(2,1)}), bf16[3712,16,32]{0,2,1:T(8,128)(2,1)}, u32[]{:S(2)}, u32[]{:S(2)}) async-start(bf16[3712,16,32]{0,2,1:T(8,128)(2,1)} %bitcast.120), calls=%async_computation | async-start | bytes 7602176 | tf_op jit(solution)/shard_map/all_to_all | solution.py:82
  63.2 2.6 scatter_custom_fusion
  67.4 77.5 %all-to-all-done = bf16[3712,16,32]{0,2,1:T(8,128)(2,1)} async-done(((bf16[3712,16,32]{0,2,1:T(8,128)(2,1)}), bf16[3712,16,32]{0,2,1:T(8,128)(2,1)}, u32[]{:S(2)}, u32[]{:S(2)}) %all-to-all-start) | async-done | bytes 3801120 | tf_op jit(solution)/shard_map/all_to_all | solution.py:82
  144.9 4.7 %gather_fusion = bf16[128,3712]{1,0:T(8,128)(2,1)S(1)} fusion(bf16[3712,512]{0,1:T(8,128)(2,1)} %bitcast.19, s32[1024]{0:T(1024)S(1)} %pad_clamp_fusion.3), kind=kCustom, calls=%fused_computation.2 | custom fusion | bytes 1901056 | tf_op jit(solution)/shard_map/jit(_take)/gather | solution.py:165
  151.5 60.9 %while.13 = (s32[]{:T(128)}, f32[2,58,32,128]{3,2,1,0:T(8,128)S(1)}, f32[1,58,1,1]{1,3,2,0:T(1,128)S(1)}, f32[2,58]{1,0:T(2,128)S(1)}, f32[2,58,128]{2,1,0:T(8,1...) while((s32[]{:T(128)}, f32[2,58,32,128]{3,2,1,0:T(8,128)S(1)}, f32[1,58,1,1]{1,3,2,0:T(1,128)S(1)}, ...), condition=%wide.region_8.10_spmd, body=%wide.region_7.9_spmd.sunk | while | flops 8315056 | bytes 25719372 | solution.py:75
  215.5 4.3 %gather_fusion.5 = bf16[512,3712]{1,0:T(8,128)(2,1)} fusion(bf16[3712,128]{0,1:T(8,128)(2,1)S(1)} %copy.83, s32[1024]{0:T(1024)S(1)} %pad_clamp_fusion.2), kind=kCustom, calls=%fused_computation.7 | custom fusion | bytes 7604224 | tf_op jit(solution)/shard_map/jit(_take)/gather | solution.py:173
  222.0 7.1 %all-to-all-start.2 = ((bf16[116,16,32]{0,2,1:T(8,128)(2,1)}), bf16[116,16,32]{0,2,1:T(8,128)(2,1)S(1)}, u32[]{:S(2)}, u32[]{:S(2)}) async-start(bf16[116,16,32]{0,2,1:T(8,128)(2,1)} %broadcast_select_fusion.3), calls=%async_computation.2 | async-start | bytes 262144 | tf_op jit(solution)/shard_map/all_to_all | solution.py:90
  229.0 4.4 %broadcast_select_fusion.1 = bf16[3712,16,32]{0,2,1:T(8,128)(2,1)} fusion(bf16[3712,16,32]{0,2,1:T(8,128)(2,1)} %bitcast.122, pred[16,32]{1,0:T(8,128)(4,1)S(1)} %compare_and_fusion), kind=kLoop, calls=%fused_computation.25 | loop fusion | flops 1900544 | bytes 7602688 | tf_op jit(solution)/shard_map/jit(_take)/select_n | solution.py:173
  234.9 6.4 %all-to-all-start.3 = ((bf16[3712,16,32]{0,2,1:T(8,128)(2,1)}), bf16[3712,16,32]{0,2,1:T(8,128)(2,1)}, u32[]{:S(2)}, u32[]{:S(2)}) async-start(bf16[3712,16,32]{0,2,1:T(8,128)(2,1)} %broadcast_select_fusion.1), calls=%async_computation.3 | async-start | bytes 7602176 | tf_op jit(solution)/shard_map/all_to_all | solution.py:89
  244.1 82.2 %collective-permute-done = f32[2,72,1,128]{3,1,2,0:T(8,128)S(1)} collective-permute-done((f32[2,72,1,128]{3,1,2,0:T(8,128)S(1)}, f32[2,72,1,128]{3,1,2,0:T(8,128)S(1)}, u32[]{:S(2)}, u32[]{:S(2)}) %collective-permute-start) | collective-permute-done | bytes 73760 | tf_op jit(solution)/shard_map/ppermute | solution.py:23
  326.3 2.0 collective-permute-done.1
  328.6 2.0 collective-permute-start.2
  331.6 2.5 collective-permute-done.3
  337.7 10.6 %gather_fusion.7 = bf16[512,3712]{1,0:T(8,128)(2,1)} fusion(bf16[3712,512]{0,1:T(8,128)(2,1)} %bitcast.41, s32[1024]{0:T(1024)S(1)} %pad_clamp_fusion), kind=kCustom, calls=%fused_computation.1.clone | custom fusion | bytes 7604224 | tf_op jit(solution)/shard_map/jit(_take)/gather | solution.py:179
  348.3 4.9 %bitcast_select_fusion = bf16[3712,512]{0,1:T(8,128)(2,1)} fusion(bf16[3712,512]{0,1:T(8,128)(2,1)} %copy.77, bf16[512,3712]{1,0:T(8,128)(2,1)} %gather_fusion.7, pred[512]{0:T(512)(128)(4,1)S(1)} %get-tuple-element.116, pred[512]{0:T(512)(128)(4,1)S(1)} %bitcast.140), kind=kLoop, calls=%fused_computation.23 | loop fusion | flops 3801088 | bytes 11404288 | tf_op jit(solution)/shard_map/jit(_where)/select_n | solution.py:182
  353.2 6.1 %copy.85 = bf16[3712,512]{1,0:T(8,128)(2,1)} copy(bf16[3712,512]{0,1:T(8,128)(2,1)} %bitcast_select_fusion) | data formatting | bytes 7602176 | tf_op jit(solution)/shard_map/jit(_where)/select_n | solution.py:182
  359.3 7.4 %reshape.504 = bf16[2,58,32,4,128]{4,3,2,1,0:T(4,128)(2,1)} reshape(bf16[3712,512]{1,0:T(8,128)(2,1)} %copy.85) | data formatting | bytes 7602176 | tf_op jit(solution)/shard_map/reshape | solution.py:182
  (290 shorter events, 87.8 us)
Async XLA Ops:
  23.4 33.4 %all-to-all-start.1 = ((bf16[144,16,32]{0,2,1:T(8,128)(2,1)}), bf16[144,16,32]{0,2,1:T(8,128)(2,1)S(1)}, u32[]{:S(2)}, u32[]{:S(2)}) async-start(bf16[144,16,32]{0,2,1:T(8,128)(2,1)} %broadcast_select_fusion.2), calls=%async_computation.1 | async-start | bytes 524288 | tf_op jit(solution)/shard_map/all_to_all | solution.py:83
  56.8 9.3 %copy-start.7 = (f32[58]{0:T(128)S(1)}, f32[58]{0:T(128)}, u32[]{:S(2)}) copy-start(f32[58]{0:T(128)} %param.20) | copy-start | bytes 700
  56.8 88.1 %all-to-all-start = ((bf16[3712,16,32]{0,2,1:T(8,128)(2,1)}), bf16[3712,16,32]{0,2,1:T(8,128)(2,1)}, u32[]{:S(2)}, u32[]{:S(2)}) async-start(bf16[3712,16,32]{0,2,1:T(8,128)(2,1)} %bitcast.120), calls=%async_computation | async-start | bytes 7602176 | tf_op jit(solution)/shard_map/all_to_all | solution.py:82
  150.8 0.7 copy-start.2
  150.8 0.7 copy-start.3
  150.8 0.7 copy-start.8
  222.0 13.0 %all-to-all-start.2 = ((bf16[116,16,32]{0,2,1:T(8,128)(2,1)}), bf16[116,16,32]{0,2,1:T(8,128)(2,1)S(1)}, u32[]{:S(2)}, u32[]{:S(2)}) async-start(bf16[116,16,32]{0,2,1:T(8,128)(2,1)} %broadcast_select_fusion.3), calls=%async_computation.2 | async-start | bytes 262144 | tf_op jit(solution)/shard_map/all_to_all | solution.py:90
  233.4 7.9 %copy-start = (f32[2,72,4,128]{3,2,1,0:T(4,128)S(1)}, f32[2,72,4,128]{3,2,1,0:T(4,128)}, u32[]{:S(2)}) copy-start(f32[2,72,4,128]{3,2,1,0:T(4,128)} %param.15) | copy-start | bytes 884740
  233.4 7.9 %copy-start.4 = (f32[4,4,1,1]{1,0,3,2:T(4,128)S(1)}, f32[4,4,1,1]{1,0,3,2:T(4,128)}, u32[]{:S(2)}) copy-start(f32[4,4,1,1]{1,0,3,2:T(4,128)} %constant.299) | copy-start | bytes 196
  233.4 8.5 %copy-start.1 = (f32[128,128,1,1]{1,0,3,2:T(8,128)S(1)}, f32[128,128,1,1]{1,0,3,2:T(8,128)}, u32[]{:S(2)}) copy-start(f32[128,128,1,1]{1,0,3,2:T(8,128)} %constant.300) | copy-start | bytes 196612
  233.4 8.5 %copy-start.5 = (f32[72]{0:T(128)S(1)}, f32[72]{0:T(128)}, u32[]{:S(2)}) copy-start(f32[72]{0:T(128)} %param.19) | copy-start | bytes 868
  233.5 8.5 %copy-start.6 = (f32[72]{0:T(128)S(1)}, f32[72]{0:T(128)}, u32[]{:S(2)}) copy-start(f32[72]{0:T(128)} %param.18) | copy-start | bytes 868
  234.9 102.8 %all-to-all-start.3 = ((bf16[3712,16,32]{0,2,1:T(8,128)(2,1)}), bf16[3712,16,32]{0,2,1:T(8,128)(2,1)}, u32[]{:S(2)}, u32[]{:S(2)}) async-start(bf16[3712,16,32]{0,2,1:T(8,128)(2,1)} %broadcast_select_fusion.1), calls=%async_computation.3 | async-start | bytes 7602176 | tf_op jit(solution)/shard_map/all_to_all | solution.py:89
  242.4 83.8 %collective-permute-start = (f32[2,72,1,128]{3,1,2,0:T(8,128)S(1)}, f32[2,72,1,128]{3,1,2,0:T(8,128)S(1)}, u32[]{:S(2)}, u32[]{:S(2)}) collective-permute-start(f32[2,72,1,128]{3,1,2,0:T(8,128)S(1)} %get-tuple-element.133), channel_id=1, source_target_pairs={{0,4},{4,8},{8,12},{12,0},{1,5},{5,9},{9,13},{13,1},{2,6},{6,10},{... | collective-permute-start | bytes 221192 | tf_op jit(solution)/shard_map/ppermute | solution.py:23
  243.7 84.6 %collective-permute-start.1 = (f32[2,72,1,128]{3,1,2,0:T(8,128)S(1)}, f32[2,72,1,128]{3,1,2,0:T(8,128)S(1)}, u32[]{:S(2)}, u32[]{:S(2)}) collective-permute-start(f32[2,72,1,128]{3,1,2,0:T(8,128)S(1)} %get-tuple-element.134), channel_id=1, source_target_pairs={{4,0},{8,4},{12,8},{0,12},{5,1},{9,5},{13,9},{1,13},{6,2},{10,6},{... | collective-permute-start | bytes 221192 | tf_op jit(solution)/shard_map/ppermute | solution.py:25
  328.6 2.8 collective-permute-start.2
  330.8 3.3 collective-permute-start.3
where the time goes:
time: 368 us; the launch traced here: 367 us
  waiting for transfers between devices  166 us (45%)
  local copies, waits for them, and re-layouts  91 us (25%)
  other arithmetic  64.7 us (18%)
  starting transfers between devices  31.1 us (8%)
  blocking collectives  8.71 us (2%)
    ppermute x2, waiting for transfers between devices, extended(): lax.ppermute(tail, axis, [(i, (i + 1) % count) for i in range(count)])  82.5 us
    all_to_all x1, waiting for transfers between devices, send_out(): lax.all_to_all(state_part, ('col', 'sub'), split_axis=1, concat_axis=1, t...  77.5 us
    add x24, other arithmetic, substep(): return current + change + jnp.stack([condense, -condense])  37.1 us
    slice x48, local copies, waits for them, and re-layouts, substep(): below = jnp.concatenate([current[:, :1], current[:, :-1]], axis=1)  11.6 us
    gather x1, local copies, waits for them, and re-layouts, body(): mine_state = jnp.take(back_state.reshape(-1, total_slots), lookup, axis=1)  10.6 us
    gather x1, local copies, waits for them, and re-layouts, body(): sent_state = jnp.take(states, source, axis=1).reshape(-1, devices, peer_cap)  10.6 us
    unnamed x1, blocking collectives  8.71 us
    unnamed x23, local copies, waits for them, and re-layouts  7.82 us
  transfers between devices with their start and end apart: 8, of which 6 were waited for; matrix products, arithmetic and copies ran while one was open for 11% of the time, Pallas kernels for 0%

commit v1 on v0

v1 whole, which is shorter than its diff:
```python
import functools

import jax
import jax.numpy as jnp
import numpy as np
from jax import lax
from jax.experimental import pallas as pl
from jax.experimental.pallas import tpu as pltpu
from jax.sharding import PartitionSpec as P

SUBSTEPS = 24
DT_DYN = 0.05
DT_CLOUD = 0.5
KAPPA = 0.15
HIGH = lax.Precision.HIGHEST
BLOCK = 8


def gll_derivative():
    nodes = np.array([-1.0, -1.0 / np.sqrt(5.0), 1.0 / np.sqrt(5.0), 1.0])
    weights = np.array(
        [1.0 / np.prod([nodes[j] - nodes[k] for k in range(4) if k != j]) for j in range(4)]
    )
    deriv = np.zeros((4, 4))
    for i in range(4):
        for j in range(4):
            if i != j:
                deriv[i, j] = weights[j] / weights[i] / (nodes[i] - nodes[j])
        deriv[i, i] = -deriv[i].sum()
    return 2.0 * deriv


def hat_rows(count_to, count_from):
    dest = (np.arange(count_to) + 0.5) / count_to
    source = (np.arange(count_from) + 0.5) / count_from
    hat = np.maximum(0.0, 1.0 - np.abs(dest[:, None] - source[None, :]) * count_from)
    hat = hat / hat.sum(axis=1, keepdims=True)
    return [[(int(c), float(row[c])) for c in np.nonzero(row > 1e-9)[0]] for row in hat]


def lanes_of(shape):
    return lax.broadcasted_iota(jnp.int32, shape, len(shape) - 1)


def rows_of(shape):
    return lax.broadcasted_iota(jnp.int32, shape, len(shape) - 2)


def tendency_kernel(levels, wind_x, wind_y, gcm, tend, first, last, ends):
    deriv = gll_derivative()
    rows, lanes = gcm.shape
    side_a, side_b = rows_of((lanes, lanes)), lanes_of((lanes, lanes))
    step_y = jnp.zeros((lanes, lanes), jnp.float32)
    for m in range(4):
        for n in range(4):
            step_y = jnp.where((side_a % 4 == m) & (side_b % 4 == n), float(deriv[n, m]), step_y)
    step_y = jnp.where(side_a // 4 == side_b // 4, step_y, 0.0)
    tend[...] = jnp.dot(gcm[...], step_y, precision=HIGH, preferred_element_type=jnp.float32)
    row = rows_of((8, lanes))
    low = row < 4
    factors = {}
    for shift in range(-3, 4):
        factor = jnp.zeros((8, lanes), jnp.float32)
        for i in range(4):
            if 0 <= i - shift < 4:
                factor = jnp.where(row % 4 == i, float(deriv[i, i - shift]), factor)
        factors[shift] = factor
    for v in range(rows // 8):
        at = slice(8 * v, 8 * v + 8)
        lev = 2 * v % levels
        here = gcm[at, :]
        along_x = factors[0] * here
        for shift in (-3, -2, -1, 1, 2, 3):
            along_x = along_x + factors[shift] * pltpu.roll(here, shift % 8, 0)
        blow_x = jnp.where(low, wind_x[lev], wind_x[lev + 1])
        blow_y = jnp.where(low, wind_y[lev], wind_y[lev + 1])
        tend[at, :] = -(blow_x * along_x + blow_y * tend[at, :])
    count = rows // 4
    first[...] = tend[pl.ds(0, count, stride=4), :]
    last[...] = tend[pl.ds(3, count, stride=4), :]
    pick = jnp.where(
        lanes_of((8, lanes)) == jnp.where(rows_of((8, lanes)) == 0, 0, lanes - 1), 1.0, 0.0
    )
    edge = lax.dot_general(
        pick, tend[...], (((1,), (1,)), ((), ())), precision=HIGH, preferred_element_type=jnp.float32
    )
    ends[:, :rows] = edge[:2]
    ends[:, rows:] = jnp.zeros((2, ends.shape[1] - rows), jnp.float32)


def dynamic_kernel(levels, cloud_levels, place, gcm, tend, before, after, ends, change, out, work):
    rows, lanes = gcm.shape
    count = rows // 4
    work[...] = tend[...]
    work[pl.ds(0, count, stride=4), :] = before[...]
    work[pl.ds(3, count, stride=4), :] = after[...]
    width = ends.shape[2]
    lane = lanes_of((2, width))

    def side(base):
        mid, low, high = ends[place[base]], ends[place[base + 1]], ends[place[base + 2]]
        other = jnp.where(
            lane % 4 == 0,
            pltpu.roll(low, width - 3, 1),
            jnp.where(lane % 4 == 3, pltpu.roll(high, 3, 1), mid),
        )
        return 0.5 * (mid + other)

    left, right = side(0), side(3)
    pair = jnp.concatenate([left[1:2], right[0:1], jnp.zeros((6, width), jnp.float32)], axis=0)
    row8, lane8 = rows_of((8, lanes)), lanes_of((8, lanes))
    spread = jnp.where((row8 < 2) & (lane8 == jnp.where(row8 == 0, 0, lanes - 1)), 1.0, 0.0)
    halo = lax.dot_general(
        pair, spread, (((0,), (0,)), ((), ())), precision=HIGH, preferred_element_type=jnp.float32
    )
    low = row8 < 4
    hats = hat_rows(levels, cloud_levels)

    def feedback(field, lev):
        total = None
        for k, weight in hats[lev]:
            term = weight * change[field, k]
            total = term if total is None else total + term
        return total

    for v in range(rows // 8):
        at = slice(8 * v, 8 * v + 8)
        field, lev = divmod(2 * v, levels)
        shared_x = 0.5 * (tend[at, :] + work[at, :])
        beside = jnp.where(
            lane8 % 4 == 0,
            pltpu.roll(shared_x, 1, 1),
            jnp.where(lane8 % 4 == 3, pltpu.roll(shared_x, lanes - 1, 1), shared_x),
        )
        beside = jnp.where((lane8 == 0) | (lane8 == lanes - 1), halo[at, :], beside)
        shared = 0.5 * (shared_x + beside)
        dynamic = gcm[at, :] + DT_DYN * shared
        out[at, :] = dynamic + jnp.where(low, feedback(field, lev), feedback(field, lev + 1))


def cloud_kernel(
    courant, relax, sat, cond_rate, gcm, active, crm, new, change,
    held, one, two, fixed, other, begin, profile, in_sem, out_sem,
):
    fields, levels, rows, lanes = crm.shape
    half_tiles = rows // 16
    tiles = rows // 8
    source_levels = profile.shape[1]
    chunk = levels // 2
    low = rows_of((8, lanes)) < 4

    def piece(f, c):
        return pl.ds(c * chunk, chunk)

    loads = [
        pltpu.make_async_copy(
            crm.at[f, pl.ds(c * chunk, chunk)], held.at[f, pl.ds(c * chunk, chunk)], in_sem.at[f, c]
        )
        for f in range(fields)
        for c in range(2)
    ]
    for load in loads:
        load.start()

    for f in range(fields):
        for v in range(source_levels // 2):
            base = (f * source_levels + 2 * v) * 4
            pair = gcm[base : base + 8, :].astype(jnp.bfloat16).astype(jnp.float32)
            swapped = pltpu.roll(pair, 4, 0)
            profile[f, 2 * v] = jnp.where(low, pair, swapped)
            profile[f, 2 * v + 1] = jnp.where(low, swapped, pair)
    for k, entries in enumerate(hat_rows(levels, source_levels)):
        for f in range(fields):
            total = None
            for l, weight in entries:
                term = weight * profile[f, l]
                total = term if total is None else total + term
            fixed[f, k] = total

    def forward(k, carry):
        ends = jnp.where((k == 0) | (k == levels - 1), KAPPA, 2.0 * KAPPA)
        result = []
        for f in range(fields):
            ratio, value = carry[f]
            rate = DT_CLOUD * relax[f, k]
            scale = 1.0 / (jnp.full((8, lanes), ends + rate, jnp.float32) - KAPPA * ratio)
            value = (rate * fixed[f, k] + KAPPA * value) * scale
            ratio = KAPPA * scale
            fixed[f, k] = value
            begin[f, k] = ratio
            result.append((ratio, value))
        return tuple(result)

    zero = jnp.zeros((8, lanes), jnp.float32)
    lax.fori_loop(0, levels, forward, tuple((zero, zero) for _ in range(fields)))

    def backward(i, carry):
        k = levels - 1 - i
        result = []
        for f in range(fields):
            value = fixed[f, k] + begin[f, k] * carry[f]
            fixed[f, k] = value
            result.append(value)
        other[k] = result[1] - sat[k]
        return tuple(result)

    lax.fori_loop(0, levels, backward, tuple(zero for _ in range(fields)))

    def unpack(f):
        def at(k, _):
            block = held[f, k].astype(jnp.float32)
            steady = fixed[f, k]
            total = zero
            for u in range(half_tiles):
                near, far = block[8 * u : 8 * u + 8], block[8 * (u + half_tiles) : 8 * (u + half_tiles) + 8]
                even = jnp.where(low, near, pltpu.roll(far, 4, 0))
                odd = jnp.where(low, pltpu.roll(near, 4, 0), far)
                total = total + (even + odd)
                one[f, k, 16 * u : 16 * u + 8, :] = even - steady
                one[f, k, 16 * u + 8 : 16 * u + 16, :] = odd - steady
            begin[f, k] = total
            return 0

        return at

    for i, load in enumerate(loads):
        load.wait()
        f, c = divmod(i, 2)
        lax.fori_loop(c * chunk, (c + 1) * chunk, unpack(f), 0)

    def advance(src, dst, first, count, scale, inverse):
        ks = [first + i for i in range(count)]
        reach = [jnp.maximum(first - 1, 0)] + ks + [jnp.minimum(first + count, levels - 1)]
        shift = [courant[k] * (1.0 / KAPPA) for k in ks]
        keep = [
            [
                (1.0 - 2.0 * KAPPA - courant[k] - DT_CLOUD * relax[f, k]) * (1.0 / KAPPA)
                for k in ks
            ]
            for f in range(fields)
        ]
        rate = [DT_CLOUD * cond_rate[k] * inverse for k in ks]
        offset = [other[k] for k in ks]
        left = [
            [pltpu.roll(src[f, k, rows - 8 : rows, :], 4, 0) for k in ks] for f in range(fields)
        ]
        for w in range(tiles):
            at = slice(8 * w, 8 * w + 8)
            here = [[src[f, k, at, :] for k in reach] for f in range(fields)]
            for i, k in enumerate(ks):
                condense = rate[i] * jnp.tanh(here[1][i + 1] * scale + offset[i])
                for f in range(fields):
                    moved = (here[f][i] + here[f][i + 2]) + (
                        keep[f][i] * here[f][i + 1] + shift[i] * left[f][i]
                    )
                    dst[f, k, at, :] = moved + condense if f == 0 else moved - condense
            left = [here[f][1:-1] for f in range(fields)]

    def substep(src, dst, scale, inverse):
        whole = levels // BLOCK

        def step(b, _):
            advance(src, dst, b * BLOCK, BLOCK, scale, inverse)
            return 0

        lax.fori_loop(0, whole, step, 0)
        if levels % BLOCK:
            advance(src, dst, whole * BLOCK, levels % BLOCK, scale, inverse)

    def two_substeps(_, carry):
        scale, inverse = carry
        substep(one, two, scale, inverse)
        scale, inverse = scale * KAPPA, inverse * (1.0 / KAPPA)
        substep(two, one, scale, inverse)
        return scale * KAPPA, inverse * (1.0 / KAPPA)

    final, _ = lax.fori_loop(
        0, SUBSTEPS // 2, two_substeps, (jnp.float32(1.0), jnp.float32(1.0 / KAPPA))
    )

    chosen = jnp.concatenate([active[...], active[...]], axis=0) > 0
    share = 2.0 / rows * 2.0

    def pack(f):
        def at(k, _):
            steady = fixed[f, k]
            block = held[f, k].astype(jnp.float32)
            total = zero
            near, far = [], []
            for u in range(half_tiles):
                even = one[f, k, 16 * u : 16 * u + 8, :] * final + steady
                odd = one[f, k, 16 * u + 8 : 16 * u + 16, :] * final + steady
                total = total + (even + odd)
                near.append(jnp.where(low, even, pltpu.roll(odd, 4, 0)))
                far.append(jnp.where(low, pltpu.roll(even, 4, 0), odd))
            tiles_new = [
                jnp.where(chosen, tile, block[8 * u : 8 * u + 8]) for u, tile in enumerate(near + far)
            ]
            held[f, k] = jnp.concatenate(tiles_new, axis=0).astype(jnp.bfloat16)
            total = total - begin[f, k]
            total = (total + pltpu.roll(total, 4, 0)) * share
            total = total.astype(jnp.bfloat16).astype(jnp.float32)
            change[f, k] = jnp.where(chosen, total, 0.0)
            return 0

        return at

    stores = []
    for f in range(fields):
        for c in range(2):
            lax.fori_loop(c * chunk, (c + 1) * chunk, pack(f), 0)
            store = pltpu.make_async_copy(
                held.at[f, pl.ds(c * chunk, chunk)], new.at[f, pl.ds(c * chunk, chunk)], out_sem.at[f, c]
            )
            store.start()
            stores.append(store)
    for store in stores:
        store.wait()


def body(gcm_state, crm_state, active, wind_x, wind_y, courant, relax, sat, cond_rate):
    fields, levels, rows_x, lanes = gcm_state.shape
    cloud_levels, cloud_columns = crm_state.shape[1:3]
    rows = fields * levels * rows_x
    gcm = gcm_state.reshape(rows, lanes)
    crm = crm_state.reshape(fields, cloud_levels, cloud_columns * rows_x, lanes)
    smem = pl.BlockSpec(memory_space=pltpu.SMEM)
    vmem = pl.BlockSpec(memory_space=pltpu.VMEM)
    anywhere = pl.BlockSpec(memory_space=pl.ANY)
    f32 = jnp.float32

    width = (rows + 127) // 128 * 128
    tend, first, last, ends = pl.pallas_call(
        functools.partial(tendency_kernel, levels),
        out_shape=(
            jax.ShapeDtypeStruct((rows, lanes), f32),
            jax.ShapeDtypeStruct((rows // rows_x, lanes), f32),
            jax.ShapeDtypeStruct((rows // rows_x, lanes), f32),
            jax.ShapeDtypeStruct((2, width), f32),
        ),
        in_specs=[smem, smem, vmem],
        out_specs=(vmem, vmem, vmem, vmem),
        name="tendency",
    )(wind_x, wind_y, gcm)

    count_x, count_y = lax.axis_size("col"), lax.axis_size("sub")
    before = lax.ppermute(last, "col", [(i, (i + 1) % count_x) for i in range(count_x)])
    after = lax.ppermute(first, "col", [((i + 1) % count_x, i) for i in range(count_x)])
    all_ends = lax.all_gather(ends, ("col", "sub"), axis=0)
    at_x, at_y = lax.axis_index("col"), lax.axis_index("sub")
    place = jnp.stack(
        [
            (at_x + dx) % count_x * count_y + (at_y + dy) % count_y
            for dy in (-1, 1)
            for dx in (0, -1, 1)
        ]
    ).astype(jnp.int32)

    slots = (fields, cloud_levels, cloud_columns * rows_x, lanes)
    new, change = pl.pallas_call(
        cloud_kernel,
        out_shape=(
            jax.ShapeDtypeStruct(slots, jnp.bfloat16),
            jax.ShapeDtypeStruct((fields, cloud_levels, 8, lanes), f32),
        ),
        in_specs=[smem, smem, smem, smem, vmem, vmem, anywhere],
        out_specs=(anywhere, vmem),
        scratch_shapes=[
            pltpu.VMEM(slots, jnp.bfloat16),
            pltpu.VMEM(slots, f32),
            pltpu.VMEM(slots, f32),
            pltpu.VMEM((fields, cloud_levels, 8, lanes), f32),
            pltpu.VMEM((cloud_levels, 8, lanes), f32),
            pltpu.VMEM((fields, cloud_levels, 8, lanes), f32),
            pltpu.VMEM((fields, levels, 8, lanes), f32),
            pltpu.SemaphoreType.DMA((fields, 2)),
            pltpu.SemaphoreType.DMA((fields, 2)),
        ],
        compiler_params=pltpu.CompilerParams(vmem_limit_bytes=48 << 20),
        cost_estimate=pl.CostEstimate(
            flops=60_000_000, bytes_accessed=200_000_000, transcendentals=20_000_000
        ),
        name="cloud",
    )(courant, relax, sat, cond_rate, gcm, active, crm)

    out = pl.pallas_call(
        functools.partial(dynamic_kernel, levels, cloud_levels),
        out_shape=jax.ShapeDtypeStruct((rows, lanes), f32),
        in_specs=[smem] + [vmem] * 6,
        out_specs=vmem,
        scratch_shapes=[pltpu.VMEM((rows, lanes), f32)],
        name="dynamic",
    )(place, gcm, tend, before, after, all_ends, change)
    return out.reshape(gcm_state.shape), new.reshape(crm_state.shape)


def solution(mesh):
    placed = (
        P(None, None, ("groups", "col"), "sub"),
        P(None, None, None, ("groups", "col"), "sub"),
        P(("groups", "col"), "sub"),
        P(),
        P(),
        P(),
        P(),
        P(),
        P(),
    )
    return jax.shard_map(
        body,
        mesh=mesh,
        in_specs=placed,
        out_specs=(
            P(None, None, ("groups", "col"), "sub"),
            P(None, None, None, ("groups", "col"), "sub"),
        ),
        check_vma=False,
    )
```

time: 368 us -> 103 us (0.28)
  the two profiles are of different devices: /device:TPU:13 before, /device:TPU:0 now
where the time goes in v1:
time: 103 us; the launch traced here: 102 us
  Pallas kernels  66.6 us (65%)
  blocking collectives  21.6 us (21%)
  local copies, waits for them, and re-layouts  8.45 us (8%)
  starting transfers between devices  5.05 us (5%)
    pallas_call x1, Pallas kernels, body(): pl.pallas_call(cloud_kernel, out_shape=(jax.ShapeDtypeStruct(slots, jnp.b...  61 us
    all_gather x1, blocking collectives, body(): all_ends = lax.all_gather(ends, ('col', 'sub'), axis=0)  21.6 us
    unnamed x22, local copies, waits for them, and re-layouts  7.78 us
    ppermute x1, starting transfers between devices, body(): lax.ppermute(last, 'col', [(i, (i + 1) % count_x) for i in range(count_x)])  3.02 us
    pallas_call x1, Pallas kernels, body(): pl.pallas_call(functools.partial(tendency_kernel, levels), out_shape=(jax...  2.97 us
    pallas_call x1, Pallas kernels, body(): pl.pallas_call(functools.partial(dynamic_kernel, levels, cloud_levels), o...  2.62 us
  transfers between devices with their start and end apart: 2, of which 0 were waited for; matrix products, arithmetic and copies ran while one was open for 1% of the time, Pallas kernels for 60%

profile of v1, /device:TPU:0, one launch (start us, length us, event | category | flops | bytes accessed | tf_op | source)
XLA Modules:
  0.0 102.4 jit_solution(6468972478428144618)
XLA Ops:
  0.6 3.0 %tendency.1 = (f32[576,128]{1,0:T(8,128)}, f32[144,128]{1,0:T(8,128)}, f32[144,128]{1,0:T(8,128)}, f32[2,640]{1,0:T(2,128)}) custom-call(f32[72]{0:T(128)} %wind_x.1, f32[72]{0:T(128)} %wind_y.1, f32[576,128]{1,0:T(8,128)} %bitcast.11), custom_call_target="tpu_custom_call" | custom-call | tf_op jit(solution)/shard_map/tendency/pallas_call | solution.py:333
  3.6 3.0 %collective-permute-start = (f32[144,128]{1,0:T(8,128)}, f32[144,128]{1,0:T(8,128)S(1)}, u32[]{:S(2)}, u32[]{:S(2)}) collective-permute-start(f32[144,128]{1,0:T(8,128)} %get-tuple-element.9), channel_id=1, source_target_pairs={{0,4},{4,8},{8,12},{12,0},{1,5},{5,9},{9,13},{13,1},{2,6},{6,10},{... | collective-permute-start | bytes 221192 | tf_op jit(solution)/shard_map/ppermute | solution.py:347
  6.6 2.0 %collective-permute-start.1 = (f32[144,128]{1,0:T(8,128)}, f32[144,128]{1,0:T(8,128)S(1)}, u32[]{:S(2)}, u32[]{:S(2)}) collective-permute-start(f32[144,128]{1,0:T(8,128)} %get-tuple-element.10), channel_id=1, source_target_pairs={{4,0},{8,4},{12,8},{0,12},{5,1},{9,5},{13,9},{1,13},{6,2},{10,6},{... | collective-permute-start | bytes 221192 | tf_op jit(solution)/shard_map/ppermute | solution.py:348
  8.7 0.7 stack.27.place
  9.3 0.0 copy-start
  9.3 1.0 copy-done
  10.3 0.0 copy-start.2
  10.3 2.1 %copy-done.2 = bf16[2,58,32,4,128]{4,3,2,1,0:T(4,128)(2,1)S(1)} copy-done((bf16[2,58,32,4,128]{4,3,2,1,0:T(4,128)(2,1)S(1)}, bf16[2,58,32,4,128]{4,3,2,1,0:T(4,128)(2,1)}, u32[]{:S(2)}) %copy-start.2) | copy-done | bytes 3801112
  12.4 0.7 copy-done.3
  13.1 0.7 copy-done.4
  13.7 0.7 copy-done.5
  14.4 0.7 copy-done.6
  15.0 0.7 copy-done.7
  15.7 61.0 %cloud.1 = (bf16[2,58,128,128]{3,2,1,0:T(8,128)(2,1)}, f32[2,58,8,128]{3,2,1,0:T(8,128)S(1)}) custom-call(f32[58]{0:T(128)S(1)} %copy-done.5, f32[2,58]{1,0:T(2,128)S(1)} %copy-done.4, f32[58]{0:T(128)S(1)} %copy-done.6, f32[58]{0:T(128)S(1)} %copy-done.7, f32[576,128]{1,0:T(8,128)S(1)} %bitcast.13, s32[4,128]{1,0:T(4,128)S(1)} %copy-done.3, ...), custom_call_target="tpu_custom_call" | custom-call | flops 60000000 | bytes 200000000 | tf_op jit(solution)/shard_map/cloud/pallas_call | solution.py:360
  76.7 0.0 copy-start.1
  76.7 0.8 copy-done.1
  77.5 0.0 copy-done.10
  77.5 21.6 %all-gather.1.ends = f32[16,2,640]{2,1,0:T(2,128)} all-gather(f32[1,2,640]{2,1,0:T(2,128)S(1)} %bitcast.16), channel_id=2, replica_groups=mesh['groups'=2,'col'=4,'sub'=4] {'col','sub'}, dimensions={0}, use_global_device_ids=true | all-gather | bytes 87040 | tf_op jit(solution)/shard_map/all_gather | solution.py:349
  99.1 0.0 collective-permute-done.before
  99.1 0.0 collective-permute-done.1.after
  99.1 0.0 copy-start.9
  99.1 0.6 copy-done.8
  99.7 0.0 copy-done.9
  99.8 2.6 %dynamic.1 = f32[576,128]{1,0:T(8,128)} custom-call(s32[6]{0:T(128)} %stack.27.place, f32[576,128]{1,0:T(8,128)} %bitcast.12, f32[576,128]{1,0:T(8,128)} %get-tuple-element.8.tend, f32[144,128]{1,0:T(8,128)} %copy-done.8, f32[144,128]{1,0:T(8,128)} %copy-done.9, f32[16,2,640]{2,1,0:T(2,128)} %all-gather.1.ends, f32[2,58,8,128]{3,2,1,0:T(8,128)} %copy-done.1), custom_call_target="tpu_custom_call" | custom-call | tf_op jit(solution)/shard_map/dynamic/pallas_call | solution.py:386
  (7 shorter events, 0.0 us)
Async XLA Ops:
  3.6 95.5 %collective-permute-start = (f32[144,128]{1,0:T(8,128)}, f32[144,128]{1,0:T(8,128)S(1)}, u32[]{:S(2)}, u32[]{:S(2)}) collective-permute-start(f32[144,128]{1,0:T(8,128)} %get-tuple-element.9), channel_id=1, source_target_pairs={{0,4},{4,8},{8,12},{12,0},{1,5},{5,9},{9,13},{13,1},{2,6},{6,10},{... | collective-permute-start | bytes 221192 | tf_op jit(solution)/shard_map/ppermute | solution.py:347
  6.6 92.5 %collective-permute-start.1 = (f32[144,128]{1,0:T(8,128)}, f32[144,128]{1,0:T(8,128)S(1)}, u32[]{:S(2)}, u32[]{:S(2)}) collective-permute-start(f32[144,128]{1,0:T(8,128)} %get-tuple-element.10), channel_id=1, source_target_pairs={{4,0},{8,4},{12,8},{0,12},{5,1},{9,5},{13,9},{1,13},{6,2},{10,6},{... | collective-permute-start | bytes 221192 | tf_op jit(solution)/shard_map/ppermute | solution.py:348
  9.3 1.0 copy-start
  10.3 2.1 %copy-start.2 = (bf16[2,58,32,4,128]{4,3,2,1,0:T(4,128)(2,1)S(1)}, bf16[2,58,32,4,128]{4,3,2,1,0:T(4,128)(2,1)}, u32[]{:S(2)}) copy-start(bf16[2,58,32,4,128]{4,3,2,1,0:T(4,128)(2,1)} %param.10) | copy-start | bytes 11403268
  12.4 0.7 copy-start.3
  13.0 0.7 copy-start.4
  13.7 0.7 copy-start.5
  14.4 0.7 copy-start.6
  15.0 0.7 copy-start.7
  15.7 61.8 %copy-start.10 = (f32[2,640]{1,0:T(2,128)S(1)}, f32[2,640]{1,0:T(2,128)}, u32[]{:S(2)}) copy-start(f32[2,640]{1,0:T(2,128)} %get-tuple-element.11) | copy-start | bytes 15364
  76.7 0.8 copy-start.1
  99.1 0.6 copy-start.8
  99.1 0.7 copy-start.9

commit v2 on v1

--- a/solution.py
+++ b/solution.py
@@ -46,7 +46,18 @@
     return lax.broadcasted_iota(jnp.int32, shape, len(shape) - 2)
 
 
-def tendency_kernel(levels, wind_x, wind_y, gcm, tend, first, last, ends):
+def fetch(pairs, sems):
+    copies = [pltpu.make_async_copy(a, b, sems.at[i]) for i, (a, b) in enumerate(pairs)]
+    for copy in copies:
+        copy.start()
+    return copies
+
+
+def tendency_kernel(
+    levels, hbm_wind_x, hbm_wind_y, hbm_gcm, tend, first, last, low_end, high_end,
+    wind_x, wind_y, gcm, sems,
+):
+    copies = fetch(((hbm_gcm, gcm), (hbm_wind_x, wind_x), (hbm_wind_y, wind_y)), sems)
     deriv = gll_derivative()
     rows, lanes = gcm.shape
     side_a, side_b = rows_of((lanes, lanes)), lanes_of((lanes, lanes))
@@ -55,6 +66,8 @@
         for n in range(4):
             step_y = jnp.where((side_a % 4 == m) & (side_b % 4 == n), float(deriv[n, m]), step_y)
     step_y = jnp.where(side_a // 4 == side_b // 4, step_y, 0.0)
+    for copy in copies:
+        copy.wait()
     tend[...] = jnp.dot(gcm[...], step_y, precision=HIGH, preferred_element_type=jnp.float32)
     row = rows_of((8, lanes))
     low = row < 4
@@ -84,21 +97,35 @@
     edge = lax.dot_general(
         pick, tend[...], (((1,), (1,)), ((), ())), precision=HIGH, preferred_element_type=jnp.float32
     )
-    ends[:, :rows] = edge[:2]
-    ends[:, rows:] = jnp.zeros((2, ends.shape[1] - rows), jnp.float32)
-
-
-def dynamic_kernel(levels, cloud_levels, place, gcm, tend, before, after, ends, change, out, work):
+    for i, end in enumerate((low_end, high_end)):
+        end[:, :rows] = edge[i : i + 1]
+        end[:, rows:] = jnp.zeros((1, end.shape[1] - rows), jnp.float32)
+
+
+def dynamic_kernel(
+    levels, cloud_levels, hbm_gcm, hbm_tend, hbm_before, hbm_after, hbm_left, hbm_left_before,
+    hbm_left_after, hbm_right, hbm_right_before, hbm_right_after, hbm_change, out,
+    gcm, tend, work, before, after, ends, change, sems,
+):
+    sides = (hbm_left, hbm_left_before, hbm_left_after, hbm_right, hbm_right_before, hbm_right_after)
+    copies = fetch(
+        ((hbm_before, before), (hbm_after, after), (hbm_tend, tend), (hbm_gcm, gcm))
+        + tuple((side, ends.at[i]) for i, side in enumerate(sides))
+        + ((hbm_change, change),),
+        sems,
+    )
+    for copy in copies:
+        copy.wait()
     rows, lanes = gcm.shape
     count = rows // 4
     work[...] = tend[...]
     work[pl.ds(0, count, stride=4), :] = before[...]
     work[pl.ds(3, count, stride=4), :] = after[...]
     width = ends.shape[2]
-    lane = lanes_of((2, width))
+    lane = lanes_of((1, width))
 
     def side(base):
-        mid, low, high = ends[place[base]], ends[place[base + 1]], ends[place[base + 2]]
+        mid, low, high = ends[base], ends[base + 1], ends[base + 2]
         other = jnp.where(
             lane % 4 == 0,
             pltpu.roll(low, width - 3, 1),
@@ -106,8 +133,7 @@
         )
         return 0.5 * (mid + other)
 
-    left, right = side(0), side(3)
-    pair = jnp.concatenate([left[1:2], right[0:1], jnp.zeros((6, width), jnp.float32)], axis=0)
+    pair = jnp.concatenate([side(0), side(3), jnp.zeros((6, width), jnp.float32)], axis=0)
     row8, lane8 = rows_of((8, lanes)), lanes_of((8, lanes))
     spread = jnp.where((row8 < 2) & (lane8 == jnp.where(row8 == 0, 0, lanes - 1)), 1.0, 0.0)
     halo = lax.dot_general(
@@ -139,9 +165,21 @@
 
 
 def cloud_kernel(
-    courant, relax, sat, cond_rate, gcm, active, crm, new, change,
-    held, one, two, fixed, other, begin, profile, in_sem, out_sem,
+    hbm_courant, hbm_relax, hbm_sat, hbm_cond, hbm_gcm, hbm_active, crm, new, change,
+    courant, relax, sat, cond_rate, gcm, active,
+    held, one, two, fixed, other, begin, profile, sems, in_sem, out_sem,
 ):
+    copies = fetch(
+        (
+            (hbm_gcm, gcm),
+            (hbm_relax, relax),
+            (hbm_sat, sat),
+            (hbm_courant, courant),
+            (hbm_cond, cond_rate),
+            (hbm_active, active),
+        ),
+        sems,
+    )
     fields, levels, rows, lanes = crm.shape
     half_tiles = rows // 16
     tiles = rows // 8
@@ -161,6 +199,8 @@
     ]
     for load in loads:
         load.start()
+    for copy in copies:
+        copy.wait()
 
     for f in range(fields):
         for v in range(source_levels // 2):
@@ -324,73 +364,104 @@
     rows = fields * levels * rows_x
     gcm = gcm_state.reshape(rows, lanes)
     crm = crm_state.reshape(fields, cloud_levels, cloud_columns * rows_x, lanes)
-    smem = pl.BlockSpec(memory_space=pltpu.SMEM)
+    def kept(*arrays):
+        return [pltpu.with_memory_space_constraint(a, pltpu.HBM) for a in arrays]
+
     vmem = pl.BlockSpec(memory_space=pltpu.VMEM)
     anywhere = pl.BlockSpec(memory_space=pl.ANY)
+    hbm = pl.BlockSpec(memory_space=pltpu.HBM)
+    dma = pltpu.SemaphoreType.DMA
     f32 = jnp.float32
-
+    count = rows // rows_x
     width = (rows + 127) // 128 * 128
-    tend, first, last, ends = pl.pallas_call(
+
+    tend, first, last, low_end, high_end = pl.pallas_call(
         functools.partial(tendency_kernel, levels),
         out_shape=(
             jax.ShapeDtypeStruct((rows, lanes), f32),
-            jax.ShapeDtypeStruct((rows // rows_x, lanes), f32),
-            jax.ShapeDtypeStruct((rows // rows_x, lanes), f32),
-            jax.ShapeDtypeStruct((2, width), f32),
+            jax.ShapeDtypeStruct((count, lanes), f32),
+            jax.ShapeDtypeStruct((count, lanes), f32),
+            jax.ShapeDtypeStruct((1, width), f32),
+            jax.ShapeDtypeStruct((1, width), f32),
         ),
-        in_specs=[smem, smem, vmem],
-        out_specs=(vmem, vmem, vmem, vmem),
+        in_specs=[hbm] * 3,
+        out_specs=(vmem,) * 5,
+        scratch_shapes=[
+            pltpu.SMEM(wind_x.shape, f32),
+            pltpu.SMEM(wind_y.shape, f32),
+            pltpu.VMEM((rows, lanes), f32),
+            dma((3,)),
+        ],
         name="tendency",
-    )(wind_x, wind_y, gcm)
+    )(*kept(wind_x, wind_y, gcm))
 
     count_x, count_y = lax.axis_size("col"), lax.axis_size("sub")
-    before = lax.ppermute(last, "col", [(i, (i + 1) % count_x) for i in range(count_x)])
-    after = lax.ppermute(first, "col", [((i + 1) % count_x, i) for i in range(count_x)])
-    all_ends = lax.all_gather(ends, ("col", "sub"), axis=0)
-    at_x, at_y = lax.axis_index("col"), lax.axis_index("sub")
-    place = jnp.stack(
-        [
-            (at_x + dx) % count_x * count_y + (at_y + dy) % count_y
-            for dy in (-1, 1)
-            for dx in (0, -1, 1)
+
+    def moved(cells, dx, dy):
+        if dy == 0:
+            return lax.ppermute(cells, "col", [(i, (i + dx) % count_x) for i in range(count_x)])
+        if dx == 0:
+            return lax.ppermute(cells, "sub", [(i, (i + dy) % count_y) for i in range(count_y)])
+        pairs = [
+            (i * count_y + j, (i + dx) % count_x * count_y + (j + dy) % count_y)
+            for i in range(count_x)
+            for j in range(count_y)
         ]
-    ).astype(jnp.int32)
+        return lax.ppermute(cells, ("col", "sub"), pairs)
+
+    before, after = moved(last, 1, 0), moved(first, -1, 0)
+    sides = [moved(high_end, dx, 1) for dx in (0, 1, -1)]
+    sides += [moved(low_end, dx, -1) for dx in (0, 1, -1)]
 
     slots = (fields, cloud_levels, cloud_columns * rows_x, lanes)
+    tile = (fields, cloud_levels, 8, lanes)
     new, change = pl.pallas_call(
         cloud_kernel,
-        out_shape=(
-            jax.ShapeDtypeStruct(slots, jnp.bfloat16),
-            jax.ShapeDtypeStruct((fields, cloud_levels, 8, lanes), f32),
-        ),
-        in_specs=[smem, smem, smem, smem, vmem, vmem, anywhere],
-        out_specs=(anywhere, vmem),
+        out_shape=(jax.ShapeDtypeStruct(slots, jnp.bfloat16), jax.ShapeDtypeStruct(tile, f32)),
+        in_specs=[hbm] * 7,
+        out_specs=(hbm, vmem),
         scratch_shapes=[
+            pltpu.SMEM(courant.shape, f32),
+            pltpu.SMEM(relax.shape, f32),
+            pltpu.SMEM(sat.shape, f32),
+            pltpu.SMEM(cond_rate.shape, f32),
+            pltpu.VMEM((rows, lanes), f32),
+            pltpu.VMEM(active.shape, active.dtype),
             pltpu.VMEM(slots, jnp.bfloat16),
             pltpu.VMEM(slots, f32),
             pltpu.VMEM(slots, f32),
-            pltpu.VMEM((fields, cloud_levels, 8, lanes), f32),
-            pltpu.VMEM((cloud_levels, 8, lanes), f32),
-            pltpu.VMEM((fields, cloud_levels, 8, lanes), f32),
+            pltpu.VMEM(tile, f32),
+            pltpu.VMEM(tile[1:], f32),
+            pltpu.VMEM(tile, f32),
             pltpu.VMEM((fields, levels, 8, lanes), f32),
-            pltpu.SemaphoreType.DMA((fields, 2)),
-            pltpu.SemaphoreType.DMA((fields, 2)),
+            dma((6,)),
+            dma((fields, 2)),
+            dma((fields, 2)),
         ],
         compiler_params=pltpu.CompilerParams(vmem_limit_bytes=48 << 20),
         cost_estimate=pl.CostEstimate(
             flops=60_000_000, bytes_accessed=200_000_000, transcendentals=20_000_000
         ),
         name="cloud",
-    )(courant, relax, sat, cond_rate, gcm, active, crm)
+    )(*kept(courant, relax, sat, cond_rate, gcm, active, crm))
 
     out = pl.pallas_call(
         functools.partial(dynamic_kernel, levels, cloud_levels),
         out_shape=jax.ShapeDtypeStruct((rows, lanes), f32),
-        in_specs=[smem] + [vmem] * 6,
+        in_specs=[hbm] + [anywhere] * 10,
         out_specs=vmem,
-        scratch_shapes=[pltpu.VMEM((rows, lanes), f32)],
+        scratch_shapes=[
+            pltpu.VMEM((rows, lanes), f32),
+            pltpu.VMEM((rows, lanes), f32),
+            pltpu.VMEM((rows, lanes), f32),
+            pltpu.VMEM((count, lanes), f32),
+            pltpu.VMEM((count, lanes), f32),
+            pltpu.VMEM((6, 1, width), f32),
+            pltpu.VMEM(tile, f32),
+            dma((11,)),
+        ],
         name="dynamic",
-    )(place, gcm, tend, before, after, all_ends, change)
+    )(*kept(gcm), tend, before, after, *sides, change)
     return out.reshape(gcm_state.shape), new.reshape(crm_state.shape)
 
 

time: 103 us -> 83.5 us (0.81)
  blocking collectives: 21.6 us -> 0 us
  starting transfers between devices: 5.05 us -> 13.1 us
  local copies, waits for them, and re-layouts: 8.45 us -> 1.42 us
  waiting for transfers between devices: 0.01 us -> 1.23 us
    all_gather x1 -> x0, blocking collectives: 21.6 us -> none  [body(): all_ends = lax.all_gather(ends, ('col', 'sub'), axis=0)]
    ppermute x2 -> x8, starting transfers between devices: 5.05 us -> 13.1 us  [the longest x4 6.23 us: moved(): return lax.ppermute(cells, ('col', 'sub'), pairs)]
    unnamed x22 -> x18, local copies, waits for them, and re-layouts: 7.78 us -> 1.42 us
    ppermute x2 -> x8, waiting for transfers between devices: 0.01 us -> 1.23 us  [the longest x4 1.22 us: moved(): return lax.ppermute(cells, ('col', 'sub'), pairs)]
  transfers between devices with their start and end apart: 2 -> 8, of which waited for: 0 -> 1; matrix products, arithmetic and copies ran while one was open for 1% -> 0% of each run, Pallas kernels for 60% -> 73%
where the time goes in v2:
time: 83.5 us; the launch traced here: 83.4 us
  Pallas kernels  66.9 us (80%)
  starting transfers between devices  13.1 us (16%)
  local copies, waits for them, and re-layouts  1.42 us (2%)
  waiting for transfers between devices  1.23 us (1%)
    pallas_call x1, Pallas kernels, body(): pl.pallas_call(cloud_kernel, out_shape=(jax.ShapeDtypeStruct(slots, jnp.b...  61.2 us
    ppermute x4, starting transfers between devices, moved(): return lax.ppermute(cells, ('col', 'sub'), pairs)  6.23 us
    ppermute x2, starting transfers between devices, moved(): lax.ppermute(cells, 'col', [(i, (i + dx) % count_x) for i in range(count_...  5.17 us
    pallas_call x1, Pallas kernels, body(): pl.pallas_call(functools.partial(tendency_kernel, levels), out_shape=(jax...  2.91 us
    pallas_call x1, Pallas kernels, body(): pl.pallas_call(functools.partial(dynamic_kernel, levels, cloud_levels), o...  2.73 us
    ppermute x2, starting transfers between devices, moved(): lax.ppermute(cells, 'sub', [(i, (i + dy) % count_y) for i in range(count_...  1.7 us
  transfers between devices with their start and end apart: 8, of which 1 were waited for; matrix products, arithmetic and copies ran while one was open for 0% of the time, Pallas kernels for 73%

profile of v2, /device:TPU:0, one launch (start us, length us, event | category | flops | bytes accessed | tf_op | source)
XLA Modules:
  0.0 83.4 jit_solution(5046614831406729003)
XLA Ops:
  0.6 2.9 %tendency.1 = (f32[576,128]{1,0:T(8,128)}, f32[144,128]{1,0:T(8,128)}, f32[144,128]{1,0:T(8,128)}, f32[1,640]{1,0:T(1,128)}, f32[1,640]{1,0:T(1,128)}) custom-call(f32[72]{0:T(128)} %hbm_wind_x.1, f32[72]{0:T(128)} %hbm_wind_y.1, f32[576,128]{1,0:T(8,128)} %bitcast.4), custom_call_target="tpu_custom_call" | custom-call | tf_op jit(solution)/shard_map/tendency/pallas_call | solution.py:378
  3.5 3.1 %collective-permute-start = (f32[144,128]{1,0:T(8,128)}, f32[144,128]{1,0:T(8,128)S(1)}, u32[]{:S(2)}, u32[]{:S(2)}) collective-permute-start(f32[144,128]{1,0:T(8,128)} %get-tuple-element.10), channel_id=1, source_target_pairs={{0,4},{4,8},{8,12},{12,0},{1,5},{5,9},{9,13},{13,1},{2,6},{6,10},{... | collective-permute-start | bytes 221192 | tf_op jit(solution)/shard_map/ppermute | solution.py:402
  6.6 2.1 %collective-permute-start.1 = (f32[144,128]{1,0:T(8,128)}, f32[144,128]{1,0:T(8,128)S(1)}, u32[]{:S(2)}, u32[]{:S(2)}) collective-permute-start(f32[144,128]{1,0:T(8,128)} %get-tuple-element.11), channel_id=1, source_target_pairs={{0,12},{4,0},{8,4},{12,8},{1,13},{5,1},{9,5},{13,9},{2,14},{6,2},{... | collective-permute-start | bytes 221192 | tf_op jit(solution)/shard_map/ppermute | solution.py:402
  8.7 0.8 %collective-permute-start.4 = (f32[1,640]{1,0:T(1,128)}, f32[1,640]{1,0:T(1,128)S(1)}, u32[]{:S(2)}, u32[]{:S(2)}) collective-permute-start(f32[1,640]{1,0:T(1,128)} %get-tuple-element.12), channel_id=1, source_target_pairs={{0,13},{1,14},{2,15},{3,12},{4,1},{5,2},{6,3},{7,0},{8,5},{9,6},{1... | collective-permute-start | bytes 7688 | tf_op jit(solution)/shard_map/ppermute | solution.py:410
  9.6 2.0 %collective-permute-start.3 = (f32[1,640]{1,0:T(1,128)}, f32[1,640]{1,0:T(1,128)S(1)}, u32[]{:S(2)}, u32[]{:S(2)}) collective-permute-start(f32[1,640]{1,0:T(1,128)} %get-tuple-element.12), channel_id=1, source_target_pairs={{0,5},{1,6},{2,7},{3,4},{4,9},{5,10},{6,11},{7,8},{8,13},{9,14},{1... | collective-permute-start | bytes 7688 | tf_op jit(solution)/shard_map/ppermute | solution.py:410
  11.5 0.2 collective-permute-start.2
  11.7 1.2 %collective-permute-done.4.hbm_left_after = f32[1,640]{1,0:T(1,128)S(1)} collective-permute-done((f32[1,640]{1,0:T(1,128)}, f32[1,640]{1,0:T(1,128)S(1)}, u32[]{:S(2)}, u32[]{:S(2)}) %collective-permute-start.4) | collective-permute-done | bytes 2592 | tf_op jit(solution)/shard_map/ppermute | solution.py:410
  12.9 3.4 %collective-permute-start.7 = (f32[1,640]{1,0:T(1,128)}, f32[1,640]{1,0:T(1,128)S(1)}, u32[]{:S(2)}, u32[]{:S(2)}) collective-permute-start(f32[1,640]{1,0:T(1,128)} %get-tuple-element.13), channel_id=1, source_target_pairs={{0,15},{1,12},{2,13},{3,14},{4,3},{5,0},{6,1},{7,2},{8,7},{9,4},{1... | collective-permute-start | bytes 7688 | tf_op jit(solution)/shard_map/ppermute | solution.py:410
  16.3 0.0 collective-permute-done.3.hbm_left_before
  16.3 0.0 collective-permute-start.6
  16.3 0.0 collective-permute-done.2.hbm_left
  16.4 1.5 %collective-permute-start.5 = (f32[1,640]{1,0:T(1,128)}, f32[1,640]{1,0:T(1,128)S(1)}, u32[]{:S(2)}, u32[]{:S(2)}) collective-permute-start(f32[1,640]{1,0:T(1,128)} %get-tuple-element.13), channel_id=1, source_target_pairs={{0,3},{1,0},{2,1},{3,2},{4,7},{5,4},{6,5},{7,6},{8,11},{9,8},{10,9... | collective-permute-start | bytes 7688 | tf_op jit(solution)/shard_map/ppermute | solution.py:404
  17.9 61.2 %cloud.1 = (bf16[2,58,128,128]{3,2,1,0:T(8,128)(2,1)}, f32[2,58,8,128]{3,2,1,0:T(8,128)S(1)}) custom-call(f32[58]{0:T(128)} %hbm_courant.1, f32[2,58]{1,0:T(2,128)} %hbm_relax.1, f32[58]{0:T(128)} %hbm_sat.1, f32[58]{0:T(128)} %hbm_cond.1, f32[576,128]{1,0:T(8,128)} %bitcast.5, s32[4,128]{1,0:T(4,128)} %hbm_active.1, bf16[2,58,128,128]{3,2,1,0:T(8,128)(2,1)} %bitcast.8), custom_call_target="tpu_custom_call" | custom-call | flops 60000000 | bytes 200000000 | tf_op jit(solution)/shard_map/cloud/pallas_call | solution.py:418
  79.2 0.8 copy-done
  79.9 0.0 collective-permute-done.7.hbm_right_after
  79.9 0.0 collective-permute-done.6.hbm_right_before
  79.9 0.0 collective-permute-done.5.hbm_right
  80.0 0.0 collective-permute-done.hbm_before
  80.0 0.5 copy-done.6
  80.5 0.0 copy-done.7
  80.5 0.0 copy-done.8
  80.5 0.1 copy-done.1
  80.6 0.0 copy-done.2
  80.6 2.7 %dynamic.1 = f32[576,128]{1,0:T(8,128)} custom-call(f32[576,128]{1,0:T(8,128)} %bitcast.6, f32[576,128]{1,0:T(8,128)} %get-tuple-element.9.hbm_tend, f32[144,128]{1,0:T(8,128)} %copy-done.1, f32[144,128]{1,0:T(8,128)} %copy-done.2, f32[1,640]{1,0:T(1,128)} %copy-done.5, f32[1,640]{1,0:T(1,128)} %copy-done.4, f32[1,640]{1,0:T(1,128)} %copy-done.3, ...), custom_call_target="tpu_custom_call" | custom-call | tf_op jit(solution)/shard_map/dynamic/pallas_call | solution.py:448
  (13 shorter events, 0.0 us)
Async XLA Ops:
  3.5 76.4 %collective-permute-start = (f32[144,128]{1,0:T(8,128)}, f32[144,128]{1,0:T(8,128)S(1)}, u32[]{:S(2)}, u32[]{:S(2)}) collective-permute-start(f32[144,128]{1,0:T(8,128)} %get-tuple-element.10), channel_id=1, source_target_pairs={{0,4},{4,8},{8,12},{12,0},{1,5},{5,9},{9,13},{13,1},{2,6},{6,10},{... | collective-permute-start | bytes 221192 | tf_op jit(solution)/shard_map/ppermute | solution.py:402
  6.6 73.4 %collective-permute-start.1 = (f32[144,128]{1,0:T(8,128)}, f32[144,128]{1,0:T(8,128)S(1)}, u32[]{:S(2)}, u32[]{:S(2)}) collective-permute-start(f32[144,128]{1,0:T(8,128)} %get-tuple-element.11), channel_id=1, source_target_pairs={{0,12},{4,0},{8,4},{12,8},{1,13},{5,1},{9,5},{13,9},{2,14},{6,2},{... | collective-permute-start | bytes 221192 | tf_op jit(solution)/shard_map/ppermute | solution.py:402
  8.7 4.2 %collective-permute-start.4 = (f32[1,640]{1,0:T(1,128)}, f32[1,640]{1,0:T(1,128)S(1)}, u32[]{:S(2)}, u32[]{:S(2)}) collective-permute-start(f32[1,640]{1,0:T(1,128)} %get-tuple-element.12), channel_id=1, source_target_pairs={{0,13},{1,14},{2,15},{3,12},{4,1},{5,2},{6,3},{7,0},{8,5},{9,6},{1... | collective-permute-start | bytes 7688 | tf_op jit(solution)/shard_map/ppermute | solution.py:410
  9.6 6.8 %collective-permute-start.3 = (f32[1,640]{1,0:T(1,128)}, f32[1,640]{1,0:T(1,128)S(1)}, u32[]{:S(2)}, u32[]{:S(2)}) collective-permute-start(f32[1,640]{1,0:T(1,128)} %get-tuple-element.12), channel_id=1, source_target_pairs={{0,5},{1,6},{2,7},{3,4},{4,9},{5,10},{6,11},{7,8},{8,13},{9,14},{1... | collective-permute-start | bytes 7688 | tf_op jit(solution)/shard_map/ppermute | solution.py:410
  11.5 4.8 %collective-permute-start.2 = (f32[1,640]{1,0:T(1,128)}, f32[1,640]{1,0:T(1,128)S(1)}, u32[]{:S(2)}, u32[]{:S(2)}) collective-permute-start(f32[1,640]{1,0:T(1,128)} %get-tuple-element.12), channel_id=1, source_target_pairs={{0,1},{1,2},{2,3},{3,0},{4,5},{5,6},{6,7},{7,4},{8,9},{9,10},{10,1... | collective-permute-start | bytes 7688 | tf_op jit(solution)/shard_map/ppermute | solution.py:404
  12.9 66.2 %copy-start.3 = (f32[1,640]{1,0:T(1,128)}, f32[1,640]{1,0:T(1,128)S(1)}, u32[]{:S(2)}) copy-start(f32[1,640]{1,0:T(1,128)S(1)} %collective-permute-done.4.hbm_left_after) | copy-start | bytes 7684
  12.9 67.0 %collective-permute-start.7 = (f32[1,640]{1,0:T(1,128)}, f32[1,640]{1,0:T(1,128)S(1)}, u32[]{:S(2)}, u32[]{:S(2)}) collective-permute-start(f32[1,640]{1,0:T(1,128)} %get-tuple-element.13), channel_id=1, source_target_pairs={{0,15},{1,12},{2,13},{3,14},{4,3},{5,0},{6,1},{7,2},{8,7},{9,4},{1... | collective-permute-start | bytes 7688 | tf_op jit(solution)/shard_map/ppermute | solution.py:410
  16.3 62.8 %copy-start.4 = (f32[1,640]{1,0:T(1,128)}, f32[1,640]{1,0:T(1,128)S(1)}, u32[]{:S(2)}) copy-start(f32[1,640]{1,0:T(1,128)S(1)} %collective-permute-done.3.hbm_left_before) | copy-start | bytes 7684
  16.3 63.6 %collective-permute-start.6 = (f32[1,640]{1,0:T(1,128)}, f32[1,640]{1,0:T(1,128)S(1)}, u32[]{:S(2)}, u32[]{:S(2)}) collective-permute-start(f32[1,640]{1,0:T(1,128)} %get-tuple-element.13), channel_id=1, source_target_pairs={{0,7},{1,4},{2,5},{3,6},{4,11},{5,8},{6,9},{7,10},{8,15},{9,12},{1... | collective-permute-start | bytes 7688 | tf_op jit(solution)/shard_map/ppermute | solution.py:410
  16.4 62.8 %copy-start.5 = (f32[1,640]{1,0:T(1,128)}, f32[1,640]{1,0:T(1,128)S(1)}, u32[]{:S(2)}) copy-start(f32[1,640]{1,0:T(1,128)S(1)} %collective-permute-done.2.hbm_left) | copy-start | bytes 7684
  16.4 63.6 %collective-permute-start.5 = (f32[1,640]{1,0:T(1,128)}, f32[1,640]{1,0:T(1,128)S(1)}, u32[]{:S(2)}, u32[]{:S(2)}) collective-permute-start(f32[1,640]{1,0:T(1,128)} %get-tuple-element.13), channel_id=1, source_target_pairs={{0,3},{1,0},{2,1},{3,2},{4,7},{5,4},{6,5},{7,6},{8,11},{9,8},{10,9... | collective-permute-start | bytes 7688 | tf_op jit(solution)/shard_map/ppermute | solution.py:404
  79.1 0.8 copy-start
  79.9 0.6 copy-start.6
  79.9 0.6 copy-start.7
  80.0 0.6 copy-start.8
  80.0 0.6 copy-start.1
  80.0 0.6 copy-start.2

commit v3 on v2

v3 whole, which is shorter than its diff:
```python
import functools

import jax
import jax.numpy as jnp
import numpy as np
from jax import lax
from jax.experimental import pallas as pl
from jax.experimental.pallas import tpu as pltpu
from jax.sharding import PartitionSpec as P

SUBSTEPS = 24
DT_DYN = 0.05
DT_CLOUD = 0.5
KAPPA = 0.15
HIGH = lax.Precision.HIGHEST
BLOCK = 8
PIECES = 4


def gll_derivative():
    nodes = np.array([-1.0, -1.0 / np.sqrt(5.0), 1.0 / np.sqrt(5.0), 1.0])
    weights = np.array(
        [1.0 / np.prod([nodes[j] - nodes[k] for k in range(4) if k != j]) for j in range(4)]
    )
    deriv = np.zeros((4, 4))
    for i in range(4):
        for j in range(4):
            if i != j:
                deriv[i, j] = weights[j] / weights[i] / (nodes[i] - nodes[j])
        deriv[i, i] = -deriv[i].sum()
    return 2.0 * deriv


def hat_rows(count_to, count_from):
    dest = (np.arange(count_to) + 0.5) / count_to
    source = (np.arange(count_from) + 0.5) / count_from
    hat = np.maximum(0.0, 1.0 - np.abs(dest[:, None] - source[None, :]) * count_from)
    hat = hat / hat.sum(axis=1, keepdims=True)
    return [[(int(c), float(row[c])) for c in np.nonzero(row > 1e-9)[0]] for row in hat]


def lanes_of(shape):
    return lax.broadcasted_iota(jnp.int32, shape, len(shape) - 1)


def rows_of(shape):
    return lax.broadcasted_iota(jnp.int32, shape, len(shape) - 2)


def fetch(pairs, sems):
    copies = [pltpu.make_async_copy(a, b, sems.at[i]) for i, (a, b) in enumerate(pairs)]
    for copy in copies:
        copy.start()
    return copies


def along_lanes(lanes):
    deriv = gll_derivative()
    side_a, side_b = rows_of((lanes, lanes)), lanes_of((lanes, lanes))
    step = jnp.zeros((lanes, lanes), jnp.float32)
    for m in range(4):
        for n in range(4):
            step = jnp.where((side_a % 4 == m) & (side_b % 4 == n), float(deriv[n, m]), step)
    return jnp.where(side_a // 4 == side_b // 4, step, 0.0)


def tendency(levels, wind_x, wind_y, gcm, tend):
    deriv = gll_derivative()
    rows, lanes = gcm.shape
    tend[...] = jnp.dot(
        gcm[...], along_lanes(lanes), precision=HIGH, preferred_element_type=jnp.float32
    )
    row = rows_of((8, lanes))
    low = row < 4
    factors = {}
    for shift in range(-3, 4):
        factor = jnp.zeros((8, lanes), jnp.float32)
        for i in range(4):
            if 0 <= i - shift < 4:
                factor = jnp.where(row % 4 == i, float(deriv[i, i - shift]), factor)
        factors[shift] = factor
    for v in range(rows // 8):
        at = slice(8 * v, 8 * v + 8)
        lev = 2 * v % levels
        here = gcm[at, :]
        along_x = factors[0] * here
        for shift in (-3, -2, -1, 1, 2, 3):
            along_x = along_x + factors[shift] * pltpu.roll(here, shift % 8, 0)
        blow_x = jnp.where(low, wind_x[lev], wind_x[lev + 1])
        blow_y = jnp.where(low, wind_y[lev], wind_y[lev + 1])
        tend[at, :] = -(blow_x * along_x + blow_y * tend[at, :])


def share_kernel(
    levels, hbm_wind_x, hbm_wind_y, hbm_before, hbm_after, hbm_tend, shared, low_end, high_end,
    wind_x, wind_y, before, after, tend, work, blow, sems,
):
    copies = fetch(
        (
            (hbm_before, before),
            (hbm_after, after),
            (hbm_tend, tend),
            (hbm_wind_x, wind_x),
            (hbm_wind_y, wind_y),
        ),
        sems,
    )
    deriv = gll_derivative()
    rows, lanes = tend.shape
    fields = rows // (4 * levels)
    step = along_lanes(lanes)
    low = rows_of((8, lanes)) < 4
    for copy in copies:
        copy.wait()
    for v in range(levels // 2):
        at = slice(8 * v, 8 * v + 8)
        blow[0, at, :] = jnp.where(low, wind_x[2 * v], wind_x[2 * v + 1])
        blow[1, at, :] = jnp.where(low, wind_y[2 * v], wind_y[2 * v + 1])
    blow_x = blow[0, pl.ds(0, levels, stride=4), :]
    blow_y = blow[1, pl.ds(0, levels, stride=4), :]
    work[...] = tend[...]
    for f in range(fields):
        for cells, node, dest in ((before, 3, 0), (after, 0, 3)):
            nodes = [cells[pl.ds(4 * levels * f + m, levels, stride=4), :] for m in range(4)]
            along_x = sum(float(deriv[node, m]) * nodes[m] for m in range(4))
            along_y = jnp.dot(
                nodes[node], step, precision=HIGH, preferred_element_type=jnp.float32
            )
            work[pl.ds(4 * levels * f + dest, levels, stride=4), :] = -(
                blow_x * along_x + blow_y * along_y
            )
    work[...] = 0.5 * (tend[...] + work[...])
    shared[...] = work[...]
    pick = jnp.where(
        lanes_of((8, lanes)) == jnp.where(rows_of((8, lanes)) == 0, 0, lanes - 1), 1.0, 0.0
    )
    edge = lax.dot_general(
        pick, work[...], (((1,), (1,)), ((), ())), precision=HIGH, preferred_element_type=jnp.float32
    )
    for i, end in enumerate((low_end, high_end)):
        end[:, :rows] = edge[i : i + 1]
        end[:, rows:] = jnp.zeros((1, end.shape[1] - rows), jnp.float32)


def dynamic_kernel(
    levels, cloud_levels, hbm_gcm, hbm_shared, hbm_left, hbm_right, hbm_change, out,
    gcm, shared, left, right, change, sems,
):
    copies = fetch(
        (
            (hbm_gcm, gcm),
            (hbm_shared, shared),
            (hbm_left, left),
            (hbm_right, right),
            (hbm_change, change),
        ),
        sems,
    )
    for copy in copies:
        copy.wait()
    rows, lanes = gcm.shape
    width = left.shape[1]
    pair = jnp.concatenate([left[...], right[...], jnp.zeros((6, width), jnp.float32)], axis=0)
    row8, lane8 = rows_of((8, lanes)), lanes_of((8, lanes))
    spread = jnp.where((row8 < 2) & (lane8 == jnp.where(row8 == 0, 0, lanes - 1)), 1.0, 0.0)
    halo = lax.dot_general(
        pair, spread, (((0,), (0,)), ((), ())), precision=HIGH, preferred_element_type=jnp.float32
    )
    low = row8 < 4
    hats = hat_rows(levels, cloud_levels)

    def feedback(field, lev):
        total = None
        for k, weight in hats[lev]:
            term = weight * change[field, k]
            total = term if total is None else total + term
        return total

    for v in range(rows // 8):
        at = slice(8 * v, 8 * v + 8)
        field, lev = divmod(2 * v, levels)
        here = shared[at, :]
        beside = jnp.where(
            lane8 % 4 == 0,
            pltpu.roll(here, 1, 1),
            jnp.where(lane8 % 4 == 3, pltpu.roll(here, lanes - 1, 1), here),
        )
        beside = jnp.where((lane8 == 0) | (lane8 == lanes - 1), halo[at, :], beside)
        dynamic = gcm[at, :] + DT_DYN * (0.5 * (here + beside))
        out[at, :] = dynamic + jnp.where(low, feedback(field, lev), feedback(field, lev + 1))


def cloud_kernel(
    hbm_courant, hbm_relax, hbm_sat, hbm_cond, hbm_gcm, hbm_active, hbm_wind_x, hbm_wind_y, crm,
    new, hbm_change, hbm_tend,
    courant, relax, sat, cond_rate, gcm, active, wind_x, wind_y, change, tend,
    held, one, two, fixed, other, begin, profile, sems, in_sem, out_sem, late_sem,
):
    copies = fetch(
        (
            (hbm_gcm, gcm),
            (hbm_relax, relax),
            (hbm_sat, sat),
            (hbm_courant, courant),
            (hbm_cond, cond_rate),
            (hbm_active, active),
            (hbm_wind_x, wind_x),
            (hbm_wind_y, wind_y),
        ),
        sems,
    )
    fields, levels, rows, lanes = crm.shape
    half_tiles = rows // 16
    tiles = rows // 8
    source_levels = profile.shape[1]
    cuts = [levels * c // (2 * PIECES) * 2 for c in range(PIECES)] + [levels]
    pieces = [pl.ds(a, b - a) for a, b in zip(cuts[:-1], cuts[1:])]
    low = rows_of((8, lanes)) < 4

    loads = [
        [
            pltpu.make_async_copy(crm.at[f, piece], held.at[f, piece], in_sem.at[f, c])
            for f in range(fields)
        ]
        for c, piece in enumerate(pieces)
    ]
    for group in loads[::-1]:
        for load in group:
            load.start()
    for copy in copies:
        copy.wait()

    for f in range(fields):
        for v in range(source_levels // 2):
            base = (f * source_levels + 2 * v) * 4
            pair = gcm[base : base + 8, :].astype(jnp.bfloat16).astype(jnp.float32)
            swapped = pltpu.roll(pair, 4, 0)
            profile[f, 2 * v] = jnp.where(low, pair, swapped)
            profile[f, 2 * v + 1] = jnp.where(low, swapped, pair)
    for k, entries in enumerate(hat_rows(levels, source_levels)):
        for f in range(fields):
            total = None
            for l, weight in entries:
                term = weight * profile[f, l]
                total = term if total is None else total + term
            fixed[f, k] = total

    zero = jnp.zeros((8, lanes), jnp.float32)
    ratio, value = [zero] * fields, [zero] * fields
    for k in range(levels):
        ends = KAPPA if k in (0, levels - 1) else 2.0 * KAPPA
        for f in range(fields):
            rate = DT_CLOUD * relax[f, k]
            scale = 1.0 / (jnp.full((8, lanes), ends + rate, jnp.float32) - KAPPA * ratio[f])
            value[f] = (rate * fixed[f, k] + KAPPA * value[f]) * scale
            ratio[f] = KAPPA * scale
            fixed[f, k] = value[f]
            begin[f, k] = ratio[f]
    tendency(source_levels, wind_x, wind_y, gcm, tend)
    late = [pltpu.make_async_copy(tend, hbm_tend, late_sem.at[0])]
    late[0].start()

    def unpack(i, carry):
        k = levels - 1 - i
        result = []
        for f in range(fields):
            steady = fixed[f, k] + begin[f, k] * carry[f]
            fixed[f, k] = steady
            result.append(steady)
            block = held[f, k].astype(jnp.float32)
            total = zero
            for u in range(half_tiles):
                near, far = (block[8 * t : 8 * t + 8] for t in (u, u + half_tiles))
                even = jnp.where(low, near, pltpu.roll(far, 4, 0))
                odd = jnp.where(low, pltpu.roll(near, 4, 0), far)
                total = total + (even + odd)
                one[f, k, 16 * u : 16 * u + 8, :] = even - steady
                one[f, k, 16 * u + 8 : 16 * u + 16, :] = odd - steady
            begin[f, k] = total
        other[k] = result[1] - sat[k]
        return tuple(result)

    carry = (zero,) * fields
    for c in range(PIECES - 1, -1, -1):
        for load in loads[c]:
            load.wait()
        first, last = levels - cuts[c + 1], levels - cuts[c]
        carry = lax.fori_loop(first, last, unpack, carry, unroll=2)

    def advance(src, dst, first, count, scale, inverse):
        ks = [first + i for i in range(count)]
        reach = [jnp.maximum(first - 1, 0)] + ks + [jnp.minimum(first + count, levels - 1)]
        shift = [courant[k] * (1.0 / KAPPA) for k in ks]
        keep = [
            [
                (1.0 - 2.0 * KAPPA - courant[k] - DT_CLOUD * relax[f, k]) * (1.0 / KAPPA)
                for k in ks
            ]
            for f in range(fields)
        ]
        rate = [DT_CLOUD * cond_rate[k] * inverse for k in ks]
        offset = [other[k] for k in ks]
        left = [
            [pltpu.roll(src[f, k, rows - 8 : rows, :], 4, 0) for k in ks] for f in range(fields)
        ]
        for w in range(tiles):
            at = slice(8 * w, 8 * w + 8)
            here = [[src[f, k, at, :] for k in reach] for f in range(fields)]
            for i, k in enumerate(ks):
                condense = rate[i] * jnp.tanh(here[1][i + 1] * scale + offset[i])
                for f in range(fields):
                    moved = (here[f][i] + here[f][i + 2]) + (
                        keep[f][i] * here[f][i + 1] + shift[i] * left[f][i]
                    )
                    dst[f, k, at, :] = moved + condense if f == 0 else moved - condense
            left = [here[f][1:-1] for f in range(fields)]

    def substep(src, dst, scale, inverse):
        whole = levels // BLOCK

        def step(b, _):
            advance(src, dst, b * BLOCK, BLOCK, scale, inverse)
            return 0

        lax.fori_loop(0, whole, step, 0)
        if levels % BLOCK:
            advance(src, dst, whole * BLOCK, levels % BLOCK, scale, inverse)

    def two_substeps(_, carry):
        scale, inverse = carry
        substep(one, two, scale, inverse)
        scale, inverse = scale * KAPPA, inverse * (1.0 / KAPPA)
        substep(two, one, scale, inverse)
        return scale * KAPPA, inverse * (1.0 / KAPPA)

    final, _ = lax.fori_loop(
        0, SUBSTEPS // 2, two_substeps, (jnp.float32(1.0), jnp.float32(1.0 / KAPPA))
    )

    chosen = jnp.concatenate([active[...], active[...]], axis=0) > 0
    chosen16 = jnp.concatenate([active[...]] * 4, axis=0).astype(jnp.bfloat16) > 0
    share = 4.0 / rows

    def pack(f):
        def at(k, _):
            steady = fixed[f, k]
            total = zero
            near, far = [], []
            for u in range(half_tiles):
                even = one[f, k, 16 * u : 16 * u + 8, :] * final + steady
                odd = one[f, k, 16 * u + 8 : 16 * u + 16, :] * final + steady
                total = total + (even + odd)
                near.append(jnp.where(low, even, pltpu.roll(odd, 4, 0)))
                far.append(jnp.where(low, pltpu.roll(even, 4, 0), odd))
            tiles_new = near + far
            for u in range(half_tiles):
                pair = jnp.concatenate(tiles_new[2 * u : 2 * u + 2], axis=0).astype(jnp.bfloat16)
                at16 = slice(16 * u, 16 * u + 16)
                held[f, k, at16, :] = jnp.where(chosen16, pair, held[f, k, at16, :])
            total = total - begin[f, k]
            total = (total + pltpu.roll(total, 4, 0)) * share
            total = total.astype(jnp.bfloat16).astype(jnp.float32)
            change[f, k] = jnp.where(chosen, total, 0.0)
            return 0

        return at

    for c, piece in enumerate(pieces):
        for f in range(fields):
            lax.fori_loop(cuts[c], cuts[c + 1], pack(f), 0, unroll=2)
            store = pltpu.make_async_copy(held.at[f, piece], new.at[f, piece], out_sem.at[f, c])
            store.start()
            late.append(store)
    store = pltpu.make_async_copy(change, hbm_change, late_sem.at[1])
    store.start()
    late.append(store)
    for store in late:
        store.wait()


def body(gcm_state, crm_state, active, wind_x, wind_y, courant, relax, sat, cond_rate):
    fields, levels, rows_x, lanes = gcm_state.shape
    cloud_levels, cloud_columns = crm_state.shape[1:3]
    rows = fields * levels * rows_x
    gcm = gcm_state.reshape(rows, lanes)
    crm = crm_state.reshape(fields, cloud_levels, cloud_columns * rows_x, lanes)
    def kept(*arrays):
        return [pltpu.with_memory_space_constraint(a, pltpu.HBM) for a in arrays]

    vmem = pl.BlockSpec(memory_space=pltpu.VMEM)
    anywhere = pl.BlockSpec(memory_space=pl.ANY)
    hbm = pl.BlockSpec(memory_space=pltpu.HBM)
    dma = pltpu.SemaphoreType.DMA
    f32 = jnp.float32
    width = (rows + 127) // 128 * 128

    def moved(cells, axis, step):
        size = lax.axis_size(axis)
        return lax.ppermute(cells, axis, [(i, (i + step) % size) for i in range(size)])

    before, after = moved(gcm, "col", 1), moved(gcm, "col", -1)

    slots = (fields, cloud_levels, cloud_columns * rows_x, lanes)
    tile = (fields, cloud_levels, 8, lanes)
    new, change, tend = pl.pallas_call(
        cloud_kernel,
        out_shape=(
            pltpu.HBM(slots, jnp.bfloat16),
            pltpu.HBM(tile, f32),
            pltpu.HBM((rows, lanes), f32),
        ),
        in_specs=[hbm] * 9,
        out_specs=(hbm,) * 3,
        scratch_shapes=[
            pltpu.SMEM(courant.shape, f32),
            pltpu.SMEM(relax.shape, f32),
            pltpu.SMEM(sat.shape, f32),
            pltpu.SMEM(cond_rate.shape, f32),
            pltpu.VMEM((rows, lanes), f32),
            pltpu.VMEM(active.shape, active.dtype),
            pltpu.SMEM(wind_x.shape, f32),
            pltpu.SMEM(wind_y.shape, f32),
            pltpu.VMEM(tile, f32),
            pltpu.VMEM((rows, lanes), f32),
            pltpu.VMEM(slots, jnp.bfloat16),
            pltpu.VMEM(slots, f32),
            pltpu.VMEM(slots, f32),
            pltpu.VMEM(tile, f32),
            pltpu.VMEM(tile[1:], f32),
            pltpu.VMEM(tile, f32),
            pltpu.VMEM((fields, levels, 8, lanes), f32),
            dma((8,)),
            dma((fields, PIECES)),
            dma((fields, PIECES)),
            dma((2,)),
        ],
        compiler_params=pltpu.CompilerParams(vmem_limit_bytes=48 << 20),
        cost_estimate=pl.CostEstimate(
            flops=60_000_000, bytes_accessed=200_000_000, transcendentals=20_000_000
        ),
        name="cloud",
    )(*kept(courant, relax, sat, cond_rate, gcm, active, wind_x, wind_y, crm))

    shared, low_end, high_end = pl.pallas_call(
        functools.partial(share_kernel, levels),
        out_shape=(
            jax.ShapeDtypeStruct((rows, lanes), f32),
            jax.ShapeDtypeStruct((1, width), f32),
            jax.ShapeDtypeStruct((1, width), f32),
        ),
        in_specs=[hbm] * 5,
        out_specs=(vmem,) * 3,
        scratch_shapes=[
            pltpu.SMEM(wind_x.shape, f32),
            pltpu.SMEM(wind_y.shape, f32),
            pltpu.VMEM((rows, lanes), f32),
            pltpu.VMEM((rows, lanes), f32),
            pltpu.VMEM((rows, lanes), f32),
            pltpu.VMEM((rows, lanes), f32),
            pltpu.VMEM((2, levels * rows_x, lanes), f32),
            dma((5,)),
        ],
        name="share",
    )(*kept(wind_x, wind_y, before, after, tend))
    left, right = moved(high_end, "sub", 1), moved(low_end, "sub", -1)

    out = pl.pallas_call(
        functools.partial(dynamic_kernel, levels, cloud_levels),
        out_shape=jax.ShapeDtypeStruct((rows, lanes), f32),
        in_specs=[hbm] + [anywhere] * 3 + [hbm],
        out_specs=vmem,
        scratch_shapes=[
            pltpu.VMEM((rows, lanes), f32),
            pltpu.VMEM((rows, lanes), f32),
            pltpu.VMEM((1, width), f32),
            pltpu.VMEM((1, width), f32),
            pltpu.VMEM(tile, f32),
            dma((5,)),
        ],
        name="dynamic",
    )(*kept(gcm), shared, left, right, *kept(change))
    return out.reshape(gcm_state.shape), new.reshape(crm_state.shape)


def solution(mesh):
    placed = (
        P(None, None, ("groups", "col"), "sub"),
        P(None, None, None, ("groups", "col"), "sub"),
        P(("groups", "col"), "sub"),
        P(),
        P(),
        P(),
        P(),
        P(),
        P(),
    )
    return jax.shard_map(
        body,
        mesh=mesh,
        in_specs=placed,
        out_specs=(
            P(None, None, ("groups", "col"), "sub"),
            P(None, None, None, ("groups", "col"), "sub"),
        ),
        check_vma=False,
    )
```

time: 83.5 us -> 76.3 us (0.914); the launches traced: 83.4 us -> 75 us
  starting transfers between devices: 13.1 us -> 6.89 us
  Pallas kernels: 66.9 us -> 64.5 us
    ppermute x8 -> x4, starting transfers between devices: 13.1 us -> 6.89 us  [moved(): lax.ppermute(cells, axis, [(i, (i + step) % size) for i in range(size)])]
    pallas_call x2, Pallas kernels: 64.1 us -> 62.1 us  [the longest x1 59.6 us: body(): pl.pallas_call(cloud_kernel, out_shape=(pltpu.HBM(slots, jnp.bfloat16), p...]
  transfers between devices with their start and end apart: 8 -> 4, of which waited for: 1 -> 1; matrix products, arithmetic and copies ran while one was open for 0% -> 0% of each run, Pallas kernels for 73% -> 79%
where the time goes in v3:
time: 76.3 us; the launch traced here: 75 us
  Pallas kernels  64.5 us (85%)
  starting transfers between devices  6.89 us (9%)
  waiting for transfers between devices  1.53 us (2%)
  local copies, waits for them, and re-layouts  1.36 us (2%)
    pallas_call x1, Pallas kernels, body(): pl.pallas_call(cloud_kernel, out_shape=(pltpu.HBM(slots, jnp.bfloat16), p...  59.6 us
    ppermute x4, starting transfers between devices, moved(): lax.ppermute(cells, axis, [(i, (i + step) % size) for i in range(size)])  6.89 us
    pallas_call x1, Pallas kernels, body(): pl.pallas_call(functools.partial(share_kernel, levels), out_shape=(jax.Sh...  2.53 us
    pallas_call x1, Pallas kernels, body(): pl.pallas_call(functools.partial(dynamic_kernel, levels, cloud_levels), o...  2.46 us
    ppermute x4, waiting for transfers between devices, moved(): lax.ppermute(cells, axis, [(i, (i + step) % size) for i in range(size)])  1.53 us
  transfers between devices with their start and end apart: 4, of which 1 were waited for; matrix products, arithmetic and copies ran while one was open for 0% of the time, Pallas kernels for 79%

profile of v3, /device:TPU:0, one launch (start us, length us, event | category | flops | bytes accessed | tf_op | source)
XLA Modules:
  0.0 75.0 jit_solution(11542082814194258645)
XLA Ops:
  0.6 5.1 %collective-permute-start.1 = (f32[576,128]{1,0:T(8,128)}, f32[576,128]{1,0:T(8,128)S(1)}, u32[]{:S(2)}, u32[]{:S(2)}) collective-permute-start(f32[576,128]{1,0:T(8,128)} %bitcast.4), channel_id=1, source_target_pairs={{0,12},{4,0},{8,4},{12,8},{1,13},{5,1},{9,5},{13,9},{2,14},{6,2},{... | collective-permute-start | bytes 884744 | tf_op jit(solution)/shard_map/ppermute | solution.py:399
  5.7 0.0 collective-permute-start
  5.7 59.6 %cloud.1 = (bf16[2,58,128,128]{3,2,1,0:T(8,128)(2,1)}, f32[2,58,8,128]{3,2,1,0:T(8,128)}, f32[576,128]{1,0:T(8,128)}) custom-call(f32[58]{0:T(128)} %hbm_courant.1, f32[2,58]{1,0:T(2,128)} %hbm_relax.1, f32[58]{0:T(128)} %hbm_sat.1, f32[58]{0:T(128)} %hbm_cond.1, f32[576,128]{1,0:T(8,128)} %bitcast.6, s32[4,128]{1,0:T(4,128)} %hbm_active.1, f32[72]{0:T(128)} %hbm_wind_x.3, ...), custom_call_target="tpu_custom_call" | custom-call | flops 60000000 | bytes 200000000 | tf_op jit(solution)/shard_map/cloud/pallas_call | solution.py:405
  65.3 0.0 collective-permute-done.1.hbm_after
  65.3 0.0 copy-start
  65.3 0.0 collective-permute-done.hbm_before
  65.3 0.0 copy-start.1
  65.3 0.7 copy-done
  66.1 0.1 copy-done.1
  66.1 2.5 %share.1 = (f32[576,128]{1,0:T(8,128)}, f32[1,640]{1,0:T(1,128)}, f32[1,640]{1,0:T(1,128)}) custom-call(f32[72]{0:T(128)} %hbm_wind_x.3, f32[72]{0:T(128)} %hbm_wind_y.3, f32[576,128]{1,0:T(8,128)} %copy-done.1, f32[576,128]{1,0:T(8,128)} %copy-done, f32[576,128]{1,0:T(8,128)} %get-tuple-element.8.hbm_tend), custom_call_target="tpu_custom_call" | custom-call | tf_op jit(solution)/shard_map/share/pallas_call | solution.py:444
  68.7 0.1 collective-permute-start.2
  68.7 1.7 %collective-permute-start.3 = (f32[1,640]{1,0:T(1,128)}, f32[1,640]{1,0:T(1,128)S(1)}, u32[]{:S(2)}, u32[]{:S(2)}) collective-permute-start(f32[1,640]{1,0:T(1,128)} %get-tuple-element.11), channel_id=1, source_target_pairs={{0,3},{1,0},{2,1},{3,2},{4,7},{5,4},{6,5},{7,6},{8,11},{9,8},{10,9... | collective-permute-start | bytes 7688 | tf_op jit(solution)/shard_map/ppermute | solution.py:399
  70.5 1.5 %collective-permute-done.2.hbm_left = f32[1,640]{1,0:T(1,128)S(1)} collective-permute-done((f32[1,640]{1,0:T(1,128)}, f32[1,640]{1,0:T(1,128)S(1)}, u32[]{:S(2)}, u32[]{:S(2)}) %collective-permute-start.2) | collective-permute-done | bytes 2592 | tf_op jit(solution)/shard_map/ppermute | solution.py:399
  71.9 0.0 copy-start.2
  71.9 0.0 collective-permute-done.3.hbm_right
  72.0 0.0 copy-start.3
  72.0 0.5 copy-done.2
  72.5 0.0 copy-done.3
  72.6 2.5 %dynamic.1 = f32[576,128]{1,0:T(8,128)} custom-call(f32[576,128]{1,0:T(8,128)} %bitcast.7, f32[576,128]{1,0:T(8,128)} %get-tuple-element.9.hbm_shared, f32[1,640]{1,0:T(1,128)} %copy-done.2, f32[1,640]{1,0:T(1,128)} %copy-done.3, f32[2,58,8,128]{3,2,1,0:T(8,128)} %get-tuple-element.12.hbm_change), custom_call_target="tpu_custom_call" | custom-call | tf_op jit(solution)/shard_map/dynamic/pallas_call | solution.py:467
Async XLA Ops:
  0.6 64.7 %collective-permute-start.1 = (f32[576,128]{1,0:T(8,128)}, f32[576,128]{1,0:T(8,128)S(1)}, u32[]{:S(2)}, u32[]{:S(2)}) collective-permute-start(f32[576,128]{1,0:T(8,128)} %bitcast.4), channel_id=1, source_target_pairs={{0,12},{4,0},{8,4},{12,8},{1,13},{5,1},{9,5},{13,9},{2,14},{6,2},{... | collective-permute-start | bytes 884744 | tf_op jit(solution)/shard_map/ppermute | solution.py:399
  5.7 59.6 %collective-permute-start = (f32[576,128]{1,0:T(8,128)}, f32[576,128]{1,0:T(8,128)S(1)}, u32[]{:S(2)}, u32[]{:S(2)}) collective-permute-start(f32[576,128]{1,0:T(8,128)} %bitcast.5), channel_id=1, source_target_pairs={{0,4},{4,8},{8,12},{12,0},{1,5},{5,9},{9,13},{13,1},{2,6},{6,10},{... | collective-permute-start | bytes 884744 | tf_op jit(solution)/shard_map/ppermute | solution.py:399
  65.3 0.7 copy-start
  65.3 0.8 %copy-start.1 = (f32[576,128]{1,0:T(8,128)}, f32[576,128]{1,0:T(8,128)S(1)}, u32[]{:S(2)}) copy-start(f32[576,128]{1,0:T(8,128)S(1)} %collective-permute-done.hbm_before) | copy-start | bytes 884740
  68.7 3.3 %collective-permute-start.2 = (f32[1,640]{1,0:T(1,128)}, f32[1,640]{1,0:T(1,128)S(1)}, u32[]{:S(2)}, u32[]{:S(2)}) collective-permute-start(f32[1,640]{1,0:T(1,128)} %get-tuple-element.10), channel_id=1, source_target_pairs={{0,1},{1,2},{2,3},{3,0},{4,5},{5,6},{6,7},{7,4},{8,9},{9,10},{10,1... | collective-permute-start | bytes 7688 | tf_op jit(solution)/shard_map/ppermute | solution.py:399
  68.7 3.3 %collective-permute-start.3 = (f32[1,640]{1,0:T(1,128)}, f32[1,640]{1,0:T(1,128)S(1)}, u32[]{:S(2)}, u32[]{:S(2)}) collective-permute-start(f32[1,640]{1,0:T(1,128)} %get-tuple-element.11), channel_id=1, source_target_pairs={{0,3},{1,0},{2,1},{3,2},{4,7},{5,4},{6,5},{7,6},{8,11},{9,8},{10,9... | collective-permute-start | bytes 7688 | tf_op jit(solution)/shard_map/ppermute | solution.py:399
  71.9 0.6 copy-start.2
  72.0 0.6 copy-start.3

commit v4 on v3

--- a/solution.py
+++ b/solution.py
@@ -13,8 +13,8 @@
 DT_CLOUD = 0.5
 KAPPA = 0.15
 HIGH = lax.Precision.HIGHEST
-BLOCK = 8
-PIECES = 4
+GROUP = 4
+PIECES = 1
 
 
 def gll_derivative():
@@ -52,6 +52,17 @@
     for copy in copies:
         copy.start()
     return copies
+
+
+def split_dot(dot, values, ones, dims):
+    ones = ones.astype(jnp.bfloat16)
+    total = None
+    for _ in range(3):
+        part = values.astype(jnp.bfloat16)
+        values = values - part.astype(jnp.float32)
+        term = dot(part, ones, dims, preferred_element_type=jnp.float32)
+        total = term if total is None else total + term
+    return total
 
 
 def along_lanes(lanes):
@@ -97,11 +108,11 @@
 ):
     copies = fetch(
         (
+            (hbm_wind_x, wind_x),
+            (hbm_wind_y, wind_y),
             (hbm_before, before),
             (hbm_after, after),
             (hbm_tend, tend),
-            (hbm_wind_x, wind_x),
-            (hbm_wind_y, wind_y),
         ),
         sems,
     )
@@ -110,7 +121,7 @@
     fields = rows // (4 * levels)
     step = along_lanes(lanes)
     low = rows_of((8, lanes)) < 4
-    for copy in copies:
+    for copy in copies[:2]:
         copy.wait()
     for v in range(levels // 2):
         at = slice(8 * v, 8 * v + 8)
@@ -118,6 +129,8 @@
         blow[1, at, :] = jnp.where(low, wind_y[2 * v], wind_y[2 * v + 1])
     blow_x = blow[0, pl.ds(0, levels, stride=4), :]
     blow_y = blow[1, pl.ds(0, levels, stride=4), :]
+    for copy in copies[2:]:
+        copy.wait()
     work[...] = tend[...]
     for f in range(fields):
         for cells, node, dest in ((before, 3, 0), (after, 0, 3)):
@@ -134,38 +147,25 @@
     pick = jnp.where(
         lanes_of((8, lanes)) == jnp.where(rows_of((8, lanes)) == 0, 0, lanes - 1), 1.0, 0.0
     )
-    edge = lax.dot_general(
-        pick, work[...], (((1,), (1,)), ((), ())), precision=HIGH, preferred_element_type=jnp.float32
+    edge = split_dot(
+        lambda a, b, dims, **kw: lax.dot_general(b, a, dims, **kw),
+        work[...], pick, (((1,), (1,)), ((), ())),
     )
     for i, end in enumerate((low_end, high_end)):
         end[:, :rows] = edge[i : i + 1]
         end[:, rows:] = jnp.zeros((1, end.shape[1] - rows), jnp.float32)
 
 
-def dynamic_kernel(
-    levels, cloud_levels, hbm_gcm, hbm_shared, hbm_left, hbm_right, hbm_change, out,
-    gcm, shared, left, right, change, sems,
+def inner_kernel(
+    levels, cloud_levels, hbm_gcm, hbm_shared, hbm_change, out, gcm, shared, change, sems
 ):
-    copies = fetch(
-        (
-            (hbm_gcm, gcm),
-            (hbm_shared, shared),
-            (hbm_left, left),
-            (hbm_right, right),
-            (hbm_change, change),
-        ),
-        sems,
-    )
+    copies = fetch(((hbm_shared, shared), (hbm_gcm, gcm), (hbm_change, change)), sems)
     for copy in copies:
         copy.wait()
     rows, lanes = gcm.shape
-    width = left.shape[1]
-    pair = jnp.concatenate([left[...], right[...], jnp.zeros((6, width), jnp.float32)], axis=0)
     row8, lane8 = rows_of((8, lanes)), lanes_of((8, lanes))
-    spread = jnp.where((row8 < 2) & (lane8 == jnp.where(row8 == 0, 0, lanes - 1)), 1.0, 0.0)
-    halo = lax.dot_general(
-        pair, spread, (((0,), (0,)), ((), ())), precision=HIGH, preferred_element_type=jnp.float32
-    )
+    first, last = lane8 % 4 == 0, lane8 % 4 == 3
+    outer = (lane8 == 0) | (lane8 == lanes - 1)
     low = row8 < 4
     hats = hat_rows(levels, cloud_levels)
 
@@ -178,23 +178,37 @@
 
     for v in range(rows // 8):
         at = slice(8 * v, 8 * v + 8)
-        field, lev = divmod(2 * v, levels)
         here = shared[at, :]
         beside = jnp.where(
-            lane8 % 4 == 0,
+            first,
             pltpu.roll(here, 1, 1),
-            jnp.where(lane8 % 4 == 3, pltpu.roll(here, lanes - 1, 1), here),
+            jnp.where(last, pltpu.roll(here, lanes - 1, 1), here),
         )
-        beside = jnp.where((lane8 == 0) | (lane8 == lanes - 1), halo[at, :], beside)
+        beside = jnp.where(outer, 0.0, beside)
+        field, lev = divmod(2 * v, levels)
         dynamic = gcm[at, :] + DT_DYN * (0.5 * (here + beside))
         out[at, :] = dynamic + jnp.where(low, feedback(field, lev), feedback(field, lev + 1))
+
+
+def outer_kernel(hbm_inner, hbm_left, hbm_right, out, inner, left, right, sems):
+    copies = fetch(((hbm_left, left), (hbm_right, right), (hbm_inner, inner)), sems)
+    for copy in copies[:2]:
+        copy.wait()
+    rows, lanes = inner.shape
+    width = left.shape[1]
+    pair = jnp.concatenate([left[...], right[...], jnp.zeros((6, width), jnp.float32)], axis=0)
+    row8, lane8 = rows_of((8, lanes)), lanes_of((8, lanes))
+    spread = jnp.where((row8 < 2) & (lane8 == jnp.where(row8 == 0, 0, lanes - 1)), 1.0, 0.0)
+    halo = split_dot(lax.dot_general, pair, spread, (((0,), (0,)), ((), ())))
+    copies[2].wait()
+    out[...] = inner[...] + (DT_DYN * 0.5) * halo[:rows]
 
 
 def cloud_kernel(
     hbm_courant, hbm_relax, hbm_sat, hbm_cond, hbm_gcm, hbm_active, hbm_wind_x, hbm_wind_y, crm,
     new, hbm_change, hbm_tend,
     courant, relax, sat, cond_rate, gcm, active, wind_x, wind_y, change, tend,
-    held, one, two, fixed, other, begin, profile, sems, in_sem, out_sem, late_sem,
+    held, one, two, fixed, other, begin, profile, factors, sems, in_sem, out_sem, late_sem,
 ):
     copies = fetch(
         (
@@ -213,18 +227,28 @@
     half_tiles = rows // 16
     tiles = rows // 8
     source_levels = profile.shape[1]
-    cuts = [levels * c // (2 * PIECES) * 2 for c in range(PIECES)] + [levels]
-    pieces = [pl.ds(a, b - a) for a, b in zip(cuts[:-1], cuts[1:])]
+    middle = levels // 2
+    cuts = [middle * c // PIECES for c in range(PIECES + 1)]
+    pieces = [
+        [
+            (f, first, b - a)
+            for first in (middle - b, middle + a)
+            for f in range(fields)
+        ]
+        for a, b in zip(cuts[:-1], cuts[1:])
+    ]
     low = rows_of((8, lanes)) < 4
 
     loads = [
         [
-            pltpu.make_async_copy(crm.at[f, piece], held.at[f, piece], in_sem.at[f, c])
-            for f in range(fields)
+            pltpu.make_async_copy(
+                crm.at[f, pl.ds(first, size)], held.at[f, pl.ds(first, size)], in_sem.at[c, i]
+            )
+            for i, (f, first, size) in enumerate(piece)
         ]
         for c, piece in enumerate(pieces)
     ]
-    for group in loads[::-1]:
+    for group in loads:
         for load in group:
             load.start()
     for copy in copies:
@@ -246,85 +270,97 @@
             fixed[f, k] = total
 
     zero = jnp.zeros((8, lanes), jnp.float32)
-    ratio, value = [zero] * fields, [zero] * fields
-    for k in range(levels):
-        ends = KAPPA if k in (0, levels - 1) else 2.0 * KAPPA
+    ratio, value = [zero] * (2 * fields), [zero] * (2 * fields)
+    for i in range(middle):
+        ends = KAPPA if i == 0 else 2.0 * KAPPA
         for f in range(fields):
-            rate = DT_CLOUD * relax[f, k]
-            scale = 1.0 / (jnp.full((8, lanes), ends + rate, jnp.float32) - KAPPA * ratio[f])
-            value[f] = (rate * fixed[f, k] + KAPPA * value[f]) * scale
-            ratio[f] = KAPPA * scale
-            fixed[f, k] = value[f]
-            begin[f, k] = ratio[f]
+            for side, k in enumerate((i, levels - 1 - i)):
+                chain = 2 * f + side
+                rate = DT_CLOUD * relax[f, k]
+                scale = 1.0 / (
+                    jnp.full((8, lanes), ends + rate, jnp.float32) - KAPPA * ratio[chain]
+                )
+                value[chain] = (rate * fixed[f, k] + KAPPA * value[chain]) * scale
+                ratio[chain] = KAPPA * scale
+                fixed[f, k] = value[chain]
+                begin[f, k] = ratio[chain]
+    carry = []
+    for f in range(fields):
+        (up_value, down_value), (up_ratio, down_ratio) = (x[2 * f : 2 * f + 2] for x in (value, ratio))
+        below = (up_value + up_ratio * down_value) / (1.0 - up_ratio * down_ratio)
+        carry += [down_value + down_ratio * below, below]
     tendency(source_levels, wind_x, wind_y, gcm, tend)
     late = [pltpu.make_async_copy(tend, hbm_tend, late_sem.at[0])]
     late[0].start()
 
     def unpack(i, carry):
-        k = levels - 1 - i
-        result = []
-        for f in range(fields):
-            steady = fixed[f, k] + begin[f, k] * carry[f]
-            fixed[f, k] = steady
-            result.append(steady)
-            block = held[f, k].astype(jnp.float32)
-            total = zero
-            for u in range(half_tiles):
-                near, far = (block[8 * t : 8 * t + 8] for t in (u, u + half_tiles))
-                even = jnp.where(low, near, pltpu.roll(far, 4, 0))
-                odd = jnp.where(low, pltpu.roll(near, 4, 0), far)
-                total = total + (even + odd)
-                one[f, k, 16 * u : 16 * u + 8, :] = even - steady
-                one[f, k, 16 * u + 8 : 16 * u + 16, :] = odd - steady
-            begin[f, k] = total
-        other[k] = result[1] - sat[k]
+        result = [None] * (2 * fields)
+        for side, k in enumerate((middle - 1 - i, middle + i)):
+            for f in range(fields):
+                steady = fixed[f, k] + begin[f, k] * carry[2 * f + side]
+                fixed[f, k] = steady
+                result[2 * f + side] = steady
+                block = held[f, k].astype(jnp.float32)
+                total = zero
+                for u in range(half_tiles):
+                    near, far = (block[8 * t : 8 * t + 8] for t in (u, u + half_tiles))
+                    even = jnp.where(low, near, pltpu.roll(far, 4, 0))
+                    odd = jnp.where(low, pltpu.roll(near, 4, 0), far)
+                    total = total + (even + odd)
+                    one[f, k, 16 * u : 16 * u + 8, :] = even - steady
+                    one[f, k, 16 * u + 8 : 16 * u + 16, :] = odd - steady
+                begin[f, k] = total
+            other[k] = result[2 + side] - sat[k]
         return tuple(result)
 
-    carry = (zero,) * fields
-    for c in range(PIECES - 1, -1, -1):
+    carry = tuple(carry)
+    for c in range(PIECES):
         for load in loads[c]:
             load.wait()
-        first, last = levels - cuts[c + 1], levels - cuts[c]
-        carry = lax.fori_loop(first, last, unpack, carry, unroll=2)
-
-    def advance(src, dst, first, count, scale, inverse):
-        ks = [first + i for i in range(count)]
-        reach = [jnp.maximum(first - 1, 0)] + ks + [jnp.minimum(first + count, levels - 1)]
-        shift = [courant[k] * (1.0 / KAPPA) for k in ks]
-        keep = [
-            [
-                (1.0 - 2.0 * KAPPA - courant[k] - DT_CLOUD * relax[f, k]) * (1.0 / KAPPA)
-                for k in ks
-            ]
-            for f in range(fields)
-        ]
-        rate = [DT_CLOUD * cond_rate[k] * inverse for k in ks]
-        offset = [other[k] for k in ks]
-        left = [
-            [pltpu.roll(src[f, k, rows - 8 : rows, :], 4, 0) for k in ks] for f in range(fields)
-        ]
-        for w in range(tiles):
-            at = slice(8 * w, 8 * w + 8)
-            here = [[src[f, k, at, :] for k in reach] for f in range(fields)]
-            for i, k in enumerate(ks):
-                condense = rate[i] * jnp.tanh(here[1][i + 1] * scale + offset[i])
-                for f in range(fields):
-                    moved = (here[f][i] + here[f][i + 2]) + (
-                        keep[f][i] * here[f][i + 1] + shift[i] * left[f][i]
-                    )
-                    dst[f, k, at, :] = moved + condense if f == 0 else moved - condense
-            left = [here[f][1:-1] for f in range(fields)]
+        carry = lax.fori_loop(cuts[c], cuts[c + 1], unpack, carry)
+
+    for k in range(levels):
+        for f in range(fields):
+            keep = (1.0 - 2.0 * KAPPA - courant[k] - DT_CLOUD * relax[f, k]) * (1.0 / KAPPA)
+            factors[f, k] = jnp.full((8, lanes), keep, jnp.float32)
+        factors[fields, k] = jnp.full((8, lanes), courant[k] * (1.0 / KAPPA), jnp.float32)
+        factors[fields + 1, k] = jnp.full((8, lanes), DT_CLOUD * cond_rate[k], jnp.float32)
 
     def substep(src, dst, scale, inverse):
-        whole = levels // BLOCK
-
-        def step(b, _):
-            advance(src, dst, b * BLOCK, BLOCK, scale, inverse)
+        for k in range(levels):
+            factors[fields + 2, k] = factors[fields + 1, k] * inverse
+
+        def group(i, _):
+            base = pl.multiple_of(i * 8 * GROUP, 8)
+            beside = pl.multiple_of(lax.rem(base + rows - 8, rows), 8)
+            turn = jnp.where(i == 0, 4, 0)
+
+            def tiles_of(f, k):
+                return [src[f, k, pl.ds(base + 8 * w, 8), :] for w in range(GROUP)]
+
+            above = [tiles_of(f, 0) for f in range(fields)]
+            here = above
+            for k in range(levels):
+                below = [tiles_of(f, min(k + 1, levels - 1)) for f in range(fields)]
+                shift, rate, offset = factors[fields, k], factors[fields + 2, k], other[k]
+                keep = [factors[f, k] for f in range(fields)]
+                left = [
+                    [pltpu.roll(src[f, k, pl.ds(beside, 8), :], turn, 0)] + here[f][:-1]
+                    for f in range(fields)
+                ]
+                for w in range(GROUP):
+                    condense = rate * jnp.tanh(here[1][w] * scale + offset)
+                    for f in range(fields):
+                        moved = (above[f][w] + below[f][w]) + (
+                            keep[f] * here[f][w] + shift * left[f][w]
+                        )
+                        dst[f, k, pl.ds(base + 8 * w, 8), :] = (
+                            moved + condense if f == 0 else moved - condense
+                        )
+                above, here = here, below
             return 0
 
-        lax.fori_loop(0, whole, step, 0)
-        if levels % BLOCK:
-            advance(src, dst, whole * BLOCK, levels % BLOCK, scale, inverse)
+        lax.fori_loop(0, tiles // GROUP, group, 0)
 
     def two_substeps(_, carry):
         scale, inverse = carry
@@ -365,12 +401,15 @@
 
         return at
 
-    for c, piece in enumerate(pieces):
-        for f in range(fields):
-            lax.fori_loop(cuts[c], cuts[c + 1], pack(f), 0, unroll=2)
-            store = pltpu.make_async_copy(held.at[f, piece], new.at[f, piece], out_sem.at[f, c])
+    for c in range(PIECES - 1, -1, -1):
+        for i, (f, first, size) in enumerate(pieces[c]):
+            lax.fori_loop(first, first + size, pack(f), 0, unroll=2)
+            store = pltpu.make_async_copy(
+                held.at[f, pl.ds(first, size)], new.at[f, pl.ds(first, size)], out_sem.at[c, i]
+            )
             store.start()
             late.append(store)
+
     store = pltpu.make_async_copy(change, hbm_change, late_sem.at[1])
     store.start()
     late.append(store)
@@ -388,7 +427,6 @@
         return [pltpu.with_memory_space_constraint(a, pltpu.HBM) for a in arrays]
 
     vmem = pl.BlockSpec(memory_space=pltpu.VMEM)
-    anywhere = pl.BlockSpec(memory_space=pl.ANY)
     hbm = pl.BlockSpec(memory_space=pltpu.HBM)
     dma = pltpu.SemaphoreType.DMA
     f32 = jnp.float32
@@ -429,12 +467,13 @@
             pltpu.VMEM(tile[1:], f32),
             pltpu.VMEM(tile, f32),
             pltpu.VMEM((fields, levels, 8, lanes), f32),
+            pltpu.VMEM((fields + 3, cloud_levels, 8, lanes), f32),
             dma((8,)),
-            dma((fields, PIECES)),
-            dma((fields, PIECES)),
+            dma((PIECES, 2 * fields)),
+            dma((PIECES, 2 * fields)),
             dma((2,)),
         ],
-        compiler_params=pltpu.CompilerParams(vmem_limit_bytes=48 << 20),
+        compiler_params=pltpu.CompilerParams(vmem_limit_bytes=(64 << 20) - (256 << 10)),
         cost_estimate=pl.CostEstimate(
             flops=60_000_000, bytes_accessed=200_000_000, transcendentals=20_000_000
         ),
@@ -464,21 +503,36 @@
     )(*kept(wind_x, wind_y, before, after, tend))
     left, right = moved(high_end, "sub", 1), moved(low_end, "sub", -1)
 
-    out = pl.pallas_call(
-        functools.partial(dynamic_kernel, levels, cloud_levels),
-        out_shape=jax.ShapeDtypeStruct((rows, lanes), f32),
-        in_specs=[hbm] + [anywhere] * 3 + [hbm],
+    inner = pl.pallas_call(
+        functools.partial(inner_kernel, levels, cloud_levels),
+        out_shape=pltpu.HBM((rows, lanes), f32),
+        in_specs=[hbm] * 3,
         out_specs=vmem,
         scratch_shapes=[
             pltpu.VMEM((rows, lanes), f32),
             pltpu.VMEM((rows, lanes), f32),
+            pltpu.VMEM(tile, f32),
+            dma((3,)),
+        ],
+        compiler_params=pltpu.CompilerParams(vmem_limit_bytes=64 << 20),
+        cost_estimate=pl.CostEstimate(
+            flops=1_000_000, bytes_accessed=5_000_000, transcendentals=0
+        ),
+        name="inner",
+    )(*kept(gcm, shared, change))
+    out = pl.pallas_call(
+        outer_kernel,
+        out_shape=jax.ShapeDtypeStruct((rows, lanes), f32),
+        in_specs=[hbm] * 3,
+        out_specs=vmem,
+        scratch_shapes=[
+            pltpu.VMEM((rows, lanes), f32),
             pltpu.VMEM((1, width), f32),
             pltpu.VMEM((1, width), f32),
-            pltpu.VMEM(tile, f32),
-            dma((5,)),
+            dma((3,)),
         ],
-        name="dynamic",
-    )(*kept(gcm), shared, left, right, *kept(change))
+        name="outer",
+    )(*kept(inner, left, right))
     return out.reshape(gcm_state.shape), new.reshape(crm_state.shape)
 
 

time: 76.3 us -> 73.1 us (0.958)
  waiting for transfers between devices: 1.53 us -> 0.01 us
  local copies, waits for them, and re-layouts: 1.36 us -> 0 us
    ppermute x4, waiting for transfers between devices: 1.53 us -> 0.01 us  [moved(): lax.ppermute(cells, axis, [(i, (i + step) % size) for i in range(size)])]
    pallas_call x1 -> x2, Pallas kernels: 2.46 us -> 3.93 us  [the longest x1 2.16 us: body(): pl.pallas_call(functools.partial(inner_kernel, levels, cloud_levels), out...]
    unnamed x8 -> x0, local copies, waits for them, and re-layouts: 1.36 us -> none
    pallas_call x1, Pallas kernels: 59.6 us -> 58.4 us  [body(): pl.pallas_call(cloud_kernel, out_shape=(pltpu.HBM(slots, jnp.bfloat16), p...]
  transfers between devices with their start and end apart: 4 -> 4, of which waited for: 1 -> 0; matrix products, arithmetic and copies ran while one was open for 0% -> 0% of each run, Pallas kernels for 79% -> 84%
where the time goes in v4:
time: 73.1 us; the launch traced here: 72.4 us
  Pallas kernels  64.8 us (89%)
  starting transfers between devices  6.89 us (9%)
    pallas_call x1, Pallas kernels, body(): pl.pallas_call(cloud_kernel, out_shape=(pltpu.HBM(slots, jnp.bfloat16), p...  58.4 us
    ppermute x4, starting transfers between devices, moved(): lax.ppermute(cells, axis, [(i, (i + step) % size) for i in range(size)])  6.89 us
    pallas_call x1, Pallas kernels, body(): pl.pallas_call(functools.partial(share_kernel, levels), out_shape=(jax.Sh...  2.45 us
    pallas_call x1, Pallas kernels, body(): pl.pallas_call(functools.partial(inner_kernel, levels, cloud_levels), out...  2.16 us
    pallas_call x1, Pallas kernels, body(): pl.pallas_call(outer_kernel, out_shape=jax.ShapeDtypeStruct((rows, lanes)...  1.77 us
  transfers between devices with their start and end apart: 4, of which 0 were waited for; matrix products, arithmetic and copies ran while one was open for 0% of the time, Pallas kernels for 84%

profile of v4, /device:TPU:0, one launch (start us, length us, event | category | flops | bytes accessed | tf_op | source)
XLA Modules:
  0.0 72.4 jit_solution(10066274025547801908)
XLA Ops:
  0.6 5.1 %collective-permute-start.1 = (f32[576,128]{1,0:T(8,128)}, f32[576,128]{1,0:T(8,128)}, u32[]{:S(2)}, u32[]{:S(2)}) collective-permute-start(f32[576,128]{1,0:T(8,128)} %bitcast.5), channel_id=1, source_target_pairs={{0,12},{4,0},{8,4},{12,8},{1,13},{5,1},{9,5},{13,9},{2,14},{6,2},{... | collective-permute-start | bytes 884744 | tf_op jit(solution)/shard_map/ppermute | solution.py:437
  5.7 0.0 collective-permute-start
  5.7 58.4 %cloud.1 = (bf16[2,58,128,128]{3,2,1,0:T(8,128)(2,1)}, f32[2,58,8,128]{3,2,1,0:T(8,128)}, f32[576,128]{1,0:T(8,128)}) custom-call(f32[58]{0:T(128)} %hbm_courant.1, f32[2,58]{1,0:T(2,128)} %hbm_relax.1, f32[58]{0:T(128)} %hbm_sat.1, f32[58]{0:T(128)} %hbm_cond.1, f32[576,128]{1,0:T(8,128)} %bitcast.7, s32[4,128]{1,0:T(4,128)} %hbm_active.1, f32[72]{0:T(128)} %hbm_wind_x.3, ...), custom_call_target="tpu_custom_call" | custom-call | flops 60000000 | bytes 200000000 | tf_op jit(solution)/shard_map/cloud/pallas_call | solution.py:443
  64.1 0.0 collective-permute-done.1.hbm_after
  64.1 0.0 collective-permute-done.hbm_before
  64.1 2.4 %share.1 = (f32[576,128]{1,0:T(8,128)}, f32[1,640]{1,0:T(1,128)}, f32[1,640]{1,0:T(1,128)}) custom-call(f32[72]{0:T(128)} %hbm_wind_x.3, f32[72]{0:T(128)} %hbm_wind_y.3, f32[576,128]{1,0:T(8,128)} %collective-permute-done.hbm_before, f32[576,128]{1,0:T(8,128)} %collective-permute-done.1.hbm_after, f32[576,128]{1,0:T(8,128)} %get-tuple-element.8.hbm_tend), custom_call_target="tpu_custom_call" | custom-call | tf_op jit(solution)/shard_map/share/pallas_call | solution.py:483
  66.6 0.1 collective-permute-start.2
  66.7 1.7 %collective-permute-start.3 = (f32[1,640]{1,0:T(1,128)}, f32[1,640]{1,0:T(1,128)}, u32[]{:S(2)}, u32[]{:S(2)}) collective-permute-start(f32[1,640]{1,0:T(1,128)} %get-tuple-element.12), channel_id=1, source_target_pairs={{0,3},{1,0},{2,1},{3,2},{4,7},{5,4},{6,5},{7,6},{8,11},{9,8},{10,9... | collective-permute-start | bytes 7688 | tf_op jit(solution)/shard_map/ppermute | solution.py:437
  68.4 2.2 %inner.1.hbm_inner = f32[576,128]{1,0:T(8,128)} custom-call(f32[576,128]{1,0:T(8,128)} %bitcast.8, f32[576,128]{1,0:T(8,128)} %get-tuple-element.9.hbm_shared, f32[2,58,8,128]{3,2,1,0:T(8,128)} %get-tuple-element.10.hbm_change), custom_call_target="tpu_custom_call" | custom-call | flops 1000000 | bytes 5000000 | tf_op jit(solution)/shard_map/inner/pallas_call | solution.py:506
  70.6 0.0 collective-permute-done.2.hbm_left
  70.6 0.0 collective-permute-done.3.hbm_right
  70.6 1.8 %outer.1 = f32[576,128]{1,0:T(8,128)} custom-call(f32[576,128]{1,0:T(8,128)} %inner.1.hbm_inner, f32[1,640]{1,0:T(1,128)} %collective-permute-done.2.hbm_left, f32[1,640]{1,0:T(1,128)} %collective-permute-done.3.hbm_right), custom_call_target="tpu_custom_call" | custom-call | tf_op jit(solution)/shard_map/outer/pallas_call | solution.py:523
Async XLA Ops:
  0.6 63.5 %collective-permute-start.1 = (f32[576,128]{1,0:T(8,128)}, f32[576,128]{1,0:T(8,128)}, u32[]{:S(2)}, u32[]{:S(2)}) collective-permute-start(f32[576,128]{1,0:T(8,128)} %bitcast.5), channel_id=1, source_target_pairs={{0,12},{4,0},{8,4},{12,8},{1,13},{5,1},{9,5},{13,9},{2,14},{6,2},{... | collective-permute-start | bytes 884744 | tf_op jit(solution)/shard_map/ppermute | solution.py:437
  5.7 58.4 %collective-permute-start = (f32[576,128]{1,0:T(8,128)}, f32[576,128]{1,0:T(8,128)}, u32[]{:S(2)}, u32[]{:S(2)}) collective-permute-start(f32[576,128]{1,0:T(8,128)} %bitcast.6), channel_id=1, source_target_pairs={{0,4},{4,8},{8,12},{12,0},{1,5},{5,9},{9,13},{13,1},{2,6},{6,10},{... | collective-permute-start | bytes 884744 | tf_op jit(solution)/shard_map/ppermute | solution.py:437
  66.6 4.0 %collective-permute-start.2 = (f32[1,640]{1,0:T(1,128)}, f32[1,640]{1,0:T(1,128)}, u32[]{:S(2)}, u32[]{:S(2)}) collective-permute-start(f32[1,640]{1,0:T(1,128)} %get-tuple-element.11), channel_id=1, source_target_pairs={{0,1},{1,2},{2,3},{3,0},{4,5},{5,6},{6,7},{7,4},{8,9},{9,10},{10,1... | collective-permute-start | bytes 7688 | tf_op jit(solution)/shard_map/ppermute | solution.py:437
  66.7 3.9 %collective-permute-start.3 = (f32[1,640]{1,0:T(1,128)}, f32[1,640]{1,0:T(1,128)}, u32[]{:S(2)}, u32[]{:S(2)}) collective-permute-start(f32[1,640]{1,0:T(1,128)} %get-tuple-element.12), channel_id=1, source_target_pairs={{0,3},{1,0},{2,1},{3,2},{4,7},{5,4},{6,5},{7,6},{8,11},{9,8},{10,9... | collective-permute-start | bytes 7688 | tf_op jit(solution)/shard_map/ppermute | solution.py:437

commit v5 on v4

--- a/solution.py
+++ b/solution.py
@@ -52,17 +52,6 @@
     for copy in copies:
         copy.start()
     return copies
-
-
-def split_dot(dot, values, ones, dims):
-    ones = ones.astype(jnp.bfloat16)
-    total = None
-    for _ in range(3):
-        part = values.astype(jnp.bfloat16)
-        values = values - part.astype(jnp.float32)
-        term = dot(part, ones, dims, preferred_element_type=jnp.float32)
-        total = term if total is None else total + term
-    return total
 
 
 def along_lanes(lanes):
@@ -103,15 +92,15 @@
 
 
 def share_kernel(
-    levels, hbm_wind_x, hbm_wind_y, hbm_before, hbm_after, hbm_tend, shared, low_end, high_end,
-    wind_x, wind_y, before, after, tend, work, blow, sems,
+    levels, hbm_wind_x, hbm_wind_y, hbm_before, hbm_after, hbm_tend, hbm_shared, hbm_end, hbm_other_end,
+    wind_x, wind_y, near, tend, work, blow, end, other_end, sems, out_sems,
 ):
     copies = fetch(
         (
             (hbm_wind_x, wind_x),
             (hbm_wind_y, wind_y),
-            (hbm_before, before),
-            (hbm_after, after),
+            (hbm_before, near.at[0]),
+            (hbm_after, near.at[1]),
             (hbm_tend, tend),
         ),
         sems,
@@ -131,29 +120,38 @@
     blow_y = blow[1, pl.ds(0, levels, stride=4), :]
     for copy in copies[2:]:
         copy.wait()
+    odd = lax.axis_index("sub") % 2
+    parts = [(f, side, node) for f in range(fields) for side, node in ((0, 3), (1, 0))]
+    nodes = [
+        [near[side, pl.ds(4 * levels * f + m, levels, stride=4), :] for m in range(4)]
+        for f, side, _ in parts
+    ]
+    along_y = jnp.dot(
+        jnp.concatenate([cells[node] for cells, (_, _, node) in zip(nodes, parts)], axis=0),
+        step,
+        precision=HIGH,
+        preferred_element_type=jnp.float32,
+    )
     work[...] = tend[...]
-    for f in range(fields):
-        for cells, node, dest in ((before, 3, 0), (after, 0, 3)):
-            nodes = [cells[pl.ds(4 * levels * f + m, levels, stride=4), :] for m in range(4)]
-            along_x = sum(float(deriv[node, m]) * nodes[m] for m in range(4))
-            along_y = jnp.dot(
-                nodes[node], step, precision=HIGH, preferred_element_type=jnp.float32
-            )
-            work[pl.ds(4 * levels * f + dest, levels, stride=4), :] = -(
-                blow_x * along_x + blow_y * along_y
-            )
-    work[...] = 0.5 * (tend[...] + work[...])
-    shared[...] = work[...]
-    pick = jnp.where(
-        lanes_of((8, lanes)) == jnp.where(rows_of((8, lanes)) == 0, 0, lanes - 1), 1.0, 0.0
-    )
-    edge = split_dot(
-        lambda a, b, dims, **kw: lax.dot_general(b, a, dims, **kw),
-        work[...], pick, (((1,), (1,)), ((), ())),
-    )
-    for i, end in enumerate((low_end, high_end)):
-        end[:, :rows] = edge[i : i + 1]
-        end[:, rows:] = jnp.zeros((1, end.shape[1] - rows), jnp.float32)
+    for i, (f, _, node) in enumerate(parts):
+        along_x = sum(float(deriv[node, m]) * nodes[i][m] for m in range(4))
+        work[pl.ds(4 * levels * f + 3 - node, levels, stride=4), :] = -(
+            blow_x * along_x + blow_y * along_y[levels * i : levels * (i + 1)]
+        )
+    lane8 = lanes_of((8, lanes))
+    low_tile = high_tile = jnp.zeros((8, lanes), jnp.float32)
+    for v in range(rows // 8):
+        at = slice(8 * v, 8 * v + 8)
+        here = 0.5 * (tend[at, :] + work[at, :])
+        work[at, :] = here
+        low_tile = jnp.where(lane8 == v, pltpu.roll(here, v, 1), low_tile)
+        high_tile = jnp.where(lane8 == v, pltpu.roll(here, (v + 1) % lanes, 1), high_tile)
+    end[...] = jnp.where(odd == 0, high_tile, low_tile)
+    other_end[...] = jnp.where(odd == 0, low_tile, high_tile)
+    for copy in fetch(
+        ((end, hbm_end), (other_end, hbm_other_end), (work, hbm_shared)), out_sems
+    ):
+        copy.wait()
 
 
 def inner_kernel(
@@ -190,18 +188,29 @@
         out[at, :] = dynamic + jnp.where(low, feedback(field, lev), feedback(field, lev + 1))
 
 
-def outer_kernel(hbm_inner, hbm_left, hbm_right, out, inner, left, right, sems):
-    copies = fetch(((hbm_left, left), (hbm_right, right), (hbm_inner, inner)), sems)
-    for copy in copies[:2]:
+def outer_kernel(
+    hbm_inner, hbm_first, hbm_second, hbm_out, inner, met, sems, out_sem
+):
+    copies = fetch(
+        ((hbm_first, met.at[0]), (hbm_second, met.at[1]), (hbm_inner, inner)), sems
+    )
+    for copy in copies:
         copy.wait()
     rows, lanes = inner.shape
-    width = left.shape[1]
-    pair = jnp.concatenate([left[...], right[...], jnp.zeros((6, width), jnp.float32)], axis=0)
-    row8, lane8 = rows_of((8, lanes)), lanes_of((8, lanes))
-    spread = jnp.where((row8 < 2) & (lane8 == jnp.where(row8 == 0, 0, lanes - 1)), 1.0, 0.0)
-    halo = split_dot(lax.dot_general, pair, spread, (((0,), (0,)), ((), ())))
-    copies[2].wait()
-    out[...] = inner[...] + (DT_DYN * 0.5) * halo[:rows]
+    lane8 = lanes_of((8, lanes))
+    odd = lax.axis_index("sub") % 2
+    at_left, at_right = met[1 - odd] * (0.5 * DT_DYN), met[odd] * (0.5 * DT_DYN)
+    for v in range(rows // 8):
+        at = slice(8 * v, 8 * v + 8)
+        halo = jnp.where(
+            lane8 == 0,
+            pltpu.roll(at_left, (lanes - v) % lanes, 1),
+            jnp.where(lane8 == lanes - 1, pltpu.roll(at_right, lanes - 1 - v, 1), 0.0),
+        )
+        inner[at, :] = inner[at, :] + halo
+    copy = pltpu.make_async_copy(inner, hbm_out, out_sem)
+    copy.start()
+    copy.wait()
 
 
 def cloud_kernel(
@@ -317,7 +326,7 @@
     for c in range(PIECES):
         for load in loads[c]:
             load.wait()
-        carry = lax.fori_loop(cuts[c], cuts[c + 1], unpack, carry)
+        carry = lax.fori_loop(cuts[c], cuts[c + 1], unpack, carry, unroll=2)
 
     for k in range(levels):
         for f in range(fields):
@@ -403,7 +412,7 @@
 
     for c in range(PIECES - 1, -1, -1):
         for i, (f, first, size) in enumerate(pieces[c]):
-            lax.fori_loop(first, first + size, pack(f), 0, unroll=2)
+            lax.fori_loop(first, first + size, pack(f), 0, unroll=4)
             store = pltpu.make_async_copy(
                 held.at[f, pl.ds(first, size)], new.at[f, pl.ds(first, size)], out_sem.at[c, i]
             )
@@ -430,13 +439,15 @@
     hbm = pl.BlockSpec(memory_space=pltpu.HBM)
     dma = pltpu.SemaphoreType.DMA
     f32 = jnp.float32
-    width = (rows + 127) // 128 * 128
-
-    def moved(cells, axis, step):
+
+    def swapped(cells, axis, first):
         size = lax.axis_size(axis)
-        return lax.ppermute(cells, axis, [(i, (i + step) % size) for i in range(size)])
-
-    before, after = moved(gcm, "col", 1), moved(gcm, "col", -1)
+        pairs = [((i + first) % size, (i + 1 + first) % size) for i in range(0, size, 2)]
+        return lax.ppermute(cells, axis, pairs + [(b, a) for a, b in pairs])
+
+    size_x = lax.axis_size("col")
+    ring = [(i, (i + 1) % size_x) for i in range(size_x)]
+    beside = lax.ppermute(gcm, "col", ring), lax.ppermute(gcm, "col", [(b, a) for a, b in ring])
 
     slots = (fields, cloud_levels, cloud_columns * rows_x, lanes)
     tile = (fields, cloud_levels, 8, lanes)
@@ -480,28 +491,30 @@
         name="cloud",
     )(*kept(courant, relax, sat, cond_rate, gcm, active, wind_x, wind_y, crm))
 
-    shared, low_end, high_end = pl.pallas_call(
+    shared, *ends = pl.pallas_call(
         functools.partial(share_kernel, levels),
         out_shape=(
-            jax.ShapeDtypeStruct((rows, lanes), f32),
-            jax.ShapeDtypeStruct((1, width), f32),
-            jax.ShapeDtypeStruct((1, width), f32),
+            pltpu.HBM((rows, lanes), f32),
+            pltpu.HBM((8, lanes), f32),
+            pltpu.HBM((8, lanes), f32),
         ),
         in_specs=[hbm] * 5,
-        out_specs=(vmem,) * 3,
+        out_specs=(hbm,) * 3,
         scratch_shapes=[
             pltpu.SMEM(wind_x.shape, f32),
             pltpu.SMEM(wind_y.shape, f32),
-            pltpu.VMEM((rows, lanes), f32),
-            pltpu.VMEM((rows, lanes), f32),
+            pltpu.VMEM((2, rows, lanes), f32),
             pltpu.VMEM((rows, lanes), f32),
             pltpu.VMEM((rows, lanes), f32),
             pltpu.VMEM((2, levels * rows_x, lanes), f32),
+            pltpu.VMEM((8, lanes), f32),
+            pltpu.VMEM((8, lanes), f32),
             dma((5,)),
+            dma((3,)),
         ],
         name="share",
-    )(*kept(wind_x, wind_y, before, after, tend))
-    left, right = moved(high_end, "sub", 1), moved(low_end, "sub", -1)
+    )(*kept(wind_x, wind_y, *beside, tend))
+    met = swapped(ends[0], "sub", 0), swapped(ends[1], "sub", 1)
 
     inner = pl.pallas_call(
         functools.partial(inner_kernel, levels, cloud_levels),
@@ -522,17 +535,17 @@
     )(*kept(gcm, shared, change))
     out = pl.pallas_call(
         outer_kernel,
-        out_shape=jax.ShapeDtypeStruct((rows, lanes), f32),
+        out_shape=pltpu.HBM((rows, lanes), f32),
         in_specs=[hbm] * 3,
-        out_specs=vmem,
+        out_specs=hbm,
         scratch_shapes=[
             pltpu.VMEM((rows, lanes), f32),
-            pltpu.VMEM((1, width), f32),
-            pltpu.VMEM((1, width), f32),
+            pltpu.VMEM((2, 8, lanes), f32),
             dma((3,)),
+            dma,
         ],
         name="outer",
-    )(*kept(inner, left, right))
+    )(*kept(inner, *met))
     return out.reshape(gcm_state.shape), new.reshape(crm_state.shape)
 
 

time: 73.1 us -> 72.2 us (0.988)
  no operation moved by 1% of the time
where the time goes in v5:
time: 72.2 us; the launch traced here: 72 us
  Pallas kernels  64.5 us (89%)
  starting transfers between devices  6.78 us (9%)
    pallas_call x1, Pallas kernels, body(): pl.pallas_call(cloud_kernel, out_shape=(pltpu.HBM(slots, jnp.bfloat16), p...  58 us
    ppermute x1, starting transfers between devices, body(): lax.ppermute(gcm, 'col', [(b, a) for a, b in ring])  5.1 us
    pallas_call x1, Pallas kernels, body(): pl.pallas_call(functools.partial(share_kernel, levels), out_shape=(pltpu....  2.41 us
    pallas_call x1, Pallas kernels, body(): pl.pallas_call(functools.partial(inner_kernel, levels, cloud_levels), out...  2.16 us
    pallas_call x1, Pallas kernels, body(): pl.pallas_call(outer_kernel, out_shape=pltpu.HBM((rows, lanes), f32), in_...  1.94 us
    ppermute x2, starting transfers between devices, swapped(): return lax.ppermute(cells, axis, pairs + [(b, a) for a, b in pairs])  1.68 us
  transfers between devices with their start and end apart: 4, of which 0 were waited for; matrix products, arithmetic and copies ran while one was open for 0% of the time, Pallas kernels for 84%

profile of v5, /device:TPU:0, one launch (start us, length us, event | category | flops | bytes accessed | tf_op | source)
XLA Modules:
  0.0 72.0 jit_solution(14628100750991992468)
XLA Ops:
  0.6 5.1 %collective-permute-start.1 = (f32[576,128]{1,0:T(8,128)}, f32[576,128]{1,0:T(8,128)}, u32[]{:S(2)}, u32[]{:S(2)}) collective-permute-start(f32[576,128]{1,0:T(8,128)} %bitcast.5), channel_id=1, source_target_pairs={{4,0},{8,4},{12,8},{0,12},{5,1},{9,5},{13,9},{1,13},{6,2},{10,6},{... | collective-permute-start | bytes 884744 | tf_op jit(solution)/shard_map/ppermute | solution.py:450
  5.7 0.0 collective-permute-start
  5.7 58.0 %cloud.1 = (bf16[2,58,128,128]{3,2,1,0:T(8,128)(2,1)}, f32[2,58,8,128]{3,2,1,0:T(8,128)}, f32[576,128]{1,0:T(8,128)}) custom-call(f32[58]{0:T(128)} %hbm_courant.1, f32[2,58]{1,0:T(2,128)} %hbm_relax.1, f32[58]{0:T(128)} %hbm_sat.1, f32[58]{0:T(128)} %hbm_cond.1, f32[576,128]{1,0:T(8,128)} %bitcast.7, s32[4,128]{1,0:T(4,128)} %hbm_active.1, f32[72]{0:T(128)} %hbm_wind_x.3, ...), custom_call_target="tpu_custom_call" | custom-call | flops 60000000 | bytes 200000000 | tf_op jit(solution)/shard_map/cloud/pallas_call | solution.py:454
  63.7 0.0 collective-permute-done.1.hbm_after
  63.7 0.0 collective-permute-done.hbm_before
  63.7 2.4 %share.1 = (f32[576,128]{1,0:T(8,128)}, f32[8,128]{1,0:T(8,128)}, f32[8,128]{1,0:T(8,128)}) custom-call(f32[72]{0:T(128)} %hbm_wind_x.3, f32[72]{0:T(128)} %hbm_wind_y.3, f32[576,128]{1,0:T(8,128)} %collective-permute-done.hbm_before, f32[576,128]{1,0:T(8,128)} %collective-permute-done.1.hbm_after, f32[576,128]{1,0:T(8,128)} %get-tuple-element.8.hbm_tend), custom_call_target="tpu_custom_call" | custom-call | tf_op jit(solution)/shard_map/share/pallas_call | solution.py:494
  66.1 0.1 collective-permute-start.2
  66.2 1.6 %collective-permute-start.3 = (f32[8,128]{1,0:T(8,128)}, f32[8,128]{1,0:T(8,128)}, u32[]{:S(2)}, u32[]{:S(2)}) collective-permute-start(f32[8,128]{1,0:T(8,128)} %get-tuple-element.12), channel_id=1, source_target_pairs={{1,2},{3,0},{2,1},{0,3},{5,6},{7,4},{6,5},{4,7},{9,10},{11,8},{10,... | collective-permute-start | bytes 12296 | tf_op jit(solution)/shard_map/ppermute | solution.py:446
  67.8 2.2 %inner.1.hbm_inner = f32[576,128]{1,0:T(8,128)} custom-call(f32[576,128]{1,0:T(8,128)} %bitcast.8, f32[576,128]{1,0:T(8,128)} %get-tuple-element.9.hbm_shared, f32[2,58,8,128]{3,2,1,0:T(8,128)} %get-tuple-element.10.hbm_change), custom_call_target="tpu_custom_call" | custom-call | flops 1000000 | bytes 5000000 | tf_op jit(solution)/shard_map/inner/pallas_call | solution.py:519
  70.0 0.0 collective-permute-done.2.hbm_first
  70.0 0.0 collective-permute-done.3.hbm_second
  70.0 1.9 %outer.1 = f32[576,128]{1,0:T(8,128)} custom-call(f32[576,128]{1,0:T(8,128)} %inner.1.hbm_inner, f32[8,128]{1,0:T(8,128)} %collective-permute-done.2.hbm_first, f32[8,128]{1,0:T(8,128)} %collective-permute-done.3.hbm_second), custom_call_target="tpu_custom_call" | custom-call | tf_op jit(solution)/shard_map/outer/pallas_call | solution.py:536
Async XLA Ops:
  0.6 63.1 %collective-permute-start.1 = (f32[576,128]{1,0:T(8,128)}, f32[576,128]{1,0:T(8,128)}, u32[]{:S(2)}, u32[]{:S(2)}) collective-permute-start(f32[576,128]{1,0:T(8,128)} %bitcast.5), channel_id=1, source_target_pairs={{4,0},{8,4},{12,8},{0,12},{5,1},{9,5},{13,9},{1,13},{6,2},{10,6},{... | collective-permute-start | bytes 884744 | tf_op jit(solution)/shard_map/ppermute | solution.py:450
  5.7 58.0 %collective-permute-start = (f32[576,128]{1,0:T(8,128)}, f32[576,128]{1,0:T(8,128)}, u32[]{:S(2)}, u32[]{:S(2)}) collective-permute-start(f32[576,128]{1,0:T(8,128)} %bitcast.6), channel_id=1, source_target_pairs={{0,4},{4,8},{8,12},{12,0},{1,5},{5,9},{9,13},{13,1},{2,6},{6,10},{... | collective-permute-start | bytes 884744 | tf_op jit(solution)/shard_map/ppermute | solution.py:450
  66.1 3.9 %collective-permute-start.2 = (f32[8,128]{1,0:T(8,128)}, f32[8,128]{1,0:T(8,128)}, u32[]{:S(2)}, u32[]{:S(2)}) collective-permute-start(f32[8,128]{1,0:T(8,128)} %get-tuple-element.11), channel_id=1, source_target_pairs={{0,1},{2,3},{1,0},{3,2},{4,5},{6,7},{5,4},{7,6},{8,9},{10,11},{9,8... | collective-permute-start | bytes 12296 | tf_op jit(solution)/shard_map/ppermute | solution.py:446
  66.2 3.8 %collective-permute-start.3 = (f32[8,128]{1,0:T(8,128)}, f32[8,128]{1,0:T(8,128)}, u32[]{:S(2)}, u32[]{:S(2)}) collective-permute-start(f32[8,128]{1,0:T(8,128)} %get-tuple-element.12), channel_id=1, source_target_pairs={{1,2},{3,0},{2,1},{0,3},{5,6},{7,4},{6,5},{4,7},{9,10},{11,8},{10,... | collective-permute-start | bytes 12296 | tf_op jit(solution)/shard_map/ppermute | solution.py:446

commit v6 on v5

--- a/solution.py
+++ b/solution.py
@@ -95,18 +95,18 @@
     levels, hbm_wind_x, hbm_wind_y, hbm_before, hbm_after, hbm_tend, hbm_shared, hbm_end, hbm_other_end,
     wind_x, wind_y, near, tend, work, blow, end, other_end, sems, out_sems,
 ):
+    rows, lanes = tend.shape
     copies = fetch(
         (
             (hbm_wind_x, wind_x),
             (hbm_wind_y, wind_y),
-            (hbm_before, near.at[0]),
-            (hbm_after, near.at[1]),
+            (hbm_before, near.at[0, pl.ds(0, rows)]),
+            (hbm_after, near.at[1, pl.ds(0, rows)]),
             (hbm_tend, tend),
         ),
         sems,
     )
     deriv = gll_derivative()
-    rows, lanes = tend.shape
     fields = rows // (4 * levels)
     step = along_lanes(lanes)
     low = rows_of((8, lanes)) < 4
@@ -132,7 +132,7 @@
         precision=HIGH,
         preferred_element_type=jnp.float32,
     )
-    work[...] = tend[...]
+    work[:rows, :] = tend[...]
     for i, (f, _, node) in enumerate(parts):
         along_x = sum(float(deriv[node, m]) * nodes[i][m] for m in range(4))
         work[pl.ds(4 * levels * f + 3 - node, levels, stride=4), :] = -(
@@ -149,7 +149,7 @@
     end[...] = jnp.where(odd == 0, high_tile, low_tile)
     other_end[...] = jnp.where(odd == 0, low_tile, high_tile)
     for copy in fetch(
-        ((end, hbm_end), (other_end, hbm_other_end), (work, hbm_shared)), out_sems
+        ((end, hbm_end), (other_end, hbm_other_end), (work.at[pl.ds(0, rows)], hbm_shared)), out_sems
     ):
         copy.wait()
 
@@ -302,6 +302,8 @@
     late = [pltpu.make_async_copy(tend, hbm_tend, late_sem.at[0])]
     late[0].start()
 
+    least = KAPPA**SUBSTEPS
+
     def unpack(i, carry):
         result = [None] * (2 * fields)
         for side, k in enumerate((middle - 1 - i, middle + i)):
@@ -316,8 +318,8 @@
                     even = jnp.where(low, near, pltpu.roll(far, 4, 0))
                     odd = jnp.where(low, pltpu.roll(near, 4, 0), far)
                     total = total + (even + odd)
-                    one[f, k, 16 * u : 16 * u + 8, :] = even - steady
-                    one[f, k, 16 * u + 8 : 16 * u + 16, :] = odd - steady
+                    one[f, k, 16 * u : 16 * u + 8, :] = (even - steady) * least
+                    one[f, k, 16 * u + 8 : 16 * u + 16, :] = (odd - steady) * least
                 begin[f, k] = total
             other[k] = result[2 + side] - sat[k]
         return tuple(result)
@@ -326,7 +328,7 @@
     for c in range(PIECES):
         for load in loads[c]:
             load.wait()
-        carry = lax.fori_loop(cuts[c], cuts[c + 1], unpack, carry, unroll=2)
+        carry = lax.fori_loop(cuts[c], cuts[c + 1], unpack, carry, unroll=4)
 
     for k in range(levels):
         for f in range(fields):
@@ -378,8 +380,8 @@
         substep(two, one, scale, inverse)
         return scale * KAPPA, inverse * (1.0 / KAPPA)
 
-    final, _ = lax.fori_loop(
-        0, SUBSTEPS // 2, two_substeps, (jnp.float32(1.0), jnp.float32(1.0 / KAPPA))
+    lax.fori_loop(
+        0, SUBSTEPS // 2, two_substeps, (jnp.float32(1.0 / least), jnp.float32(least / KAPPA))
     )
 
     chosen = jnp.concatenate([active[...], active[...]], axis=0) > 0
@@ -392,8 +394,8 @@
             total = zero
             near, far = [], []
             for u in range(half_tiles):
-                even = one[f, k, 16 * u : 16 * u + 8, :] * final + steady
-                odd = one[f, k, 16 * u + 8 : 16 * u + 16, :] * final + steady
+                even = one[f, k, 16 * u : 16 * u + 8, :] + steady
+                odd = one[f, k, 16 * u + 8 : 16 * u + 16, :] + steady
                 total = total + (even + odd)
                 near.append(jnp.where(low, even, pltpu.roll(odd, 4, 0)))
                 far.append(jnp.where(low, pltpu.roll(even, 4, 0), odd))
@@ -503,10 +505,10 @@
         scratch_shapes=[
             pltpu.SMEM(wind_x.shape, f32),
             pltpu.SMEM(wind_y.shape, f32),
-            pltpu.VMEM((2, rows, lanes), f32),
+            pltpu.VMEM((2, rows + 8, lanes), f32),
             pltpu.VMEM((rows, lanes), f32),
-            pltpu.VMEM((rows, lanes), f32),
-            pltpu.VMEM((2, levels * rows_x, lanes), f32),
+            pltpu.VMEM((rows + 8, lanes), f32),
+            pltpu.VMEM((2, levels * rows_x + 8, lanes), f32),
             pltpu.VMEM((8, lanes), f32),
             pltpu.VMEM((8, lanes), f32),
             dma((5,)),

time: 72.2 us -> 72.1 us (level)
  no operation moved by 1% of the time
where the time goes in v6:
time: 72.1 us; the launch traced here: 71.9 us
  Pallas kernels  64.4 us (89%)
  starting transfers between devices  6.78 us (9%)
    pallas_call x1, Pallas kernels, body(): pl.pallas_call(cloud_kernel, out_shape=(pltpu.HBM(slots, jnp.bfloat16), p...  57.9 us
    ppermute x1, starting transfers between devices, body(): lax.ppermute(gcm, 'col', [(b, a) for a, b in ring])  5.1 us
    pallas_call x1, Pallas kernels, body(): pl.pallas_call(functools.partial(share_kernel, levels), out_shape=(pltpu....  2.41 us
    pallas_call x1, Pallas kernels, body(): pl.pallas_call(functools.partial(inner_kernel, levels, cloud_levels), out...  2.16 us
    pallas_call x1, Pallas kernels, body(): pl.pallas_call(outer_kernel, out_shape=pltpu.HBM((rows, lanes), f32), in_...  1.94 us
    ppermute x2, starting transfers between devices, swapped(): return lax.ppermute(cells, axis, pairs + [(b, a) for a, b in pairs])  1.67 us
  transfers between devices with their start and end apart: 4, of which 0 were waited for; matrix products, arithmetic and copies ran while one was open for 0% of the time, Pallas kernels for 84%

profile of v6, /device:TPU:0, one launch (start us, length us, event | category | flops | bytes accessed | tf_op | source)
XLA Modules:
  0.0 71.9 jit_solution(11643258468476353056)
XLA Ops:
  0.6 5.1 %collective-permute-start.1 = (f32[576,128]{1,0:T(8,128)}, f32[576,128]{1,0:T(8,128)}, u32[]{:S(2)}, u32[]{:S(2)}) collective-permute-start(f32[576,128]{1,0:T(8,128)} %bitcast.5), channel_id=1, source_target_pairs={{4,0},{8,4},{12,8},{0,12},{5,1},{9,5},{13,9},{1,13},{6,2},{10,6},{... | collective-permute-start | bytes 884744 | tf_op jit(solution)/shard_map/ppermute | solution.py:452
  5.7 0.0 collective-permute-start
  5.7 57.9 %cloud.1 = (bf16[2,58,128,128]{3,2,1,0:T(8,128)(2,1)}, f32[2,58,8,128]{3,2,1,0:T(8,128)}, f32[576,128]{1,0:T(8,128)}) custom-call(f32[58]{0:T(128)} %hbm_courant.1, f32[2,58]{1,0:T(2,128)} %hbm_relax.1, f32[58]{0:T(128)} %hbm_sat.1, f32[58]{0:T(128)} %hbm_cond.1, f32[576,128]{1,0:T(8,128)} %bitcast.7, s32[4,128]{1,0:T(4,128)} %hbm_active.1, f32[72]{0:T(128)} %hbm_wind_x.3, ...), custom_call_target="tpu_custom_call" | custom-call | flops 60000000 | bytes 200000000 | tf_op jit(solution)/shard_map/cloud/pallas_call | solution.py:456
  63.6 0.0 collective-permute-done.1.hbm_after
  63.6 0.0 collective-permute-done.hbm_before
  63.6 2.4 %share.1 = (f32[576,128]{1,0:T(8,128)}, f32[8,128]{1,0:T(8,128)}, f32[8,128]{1,0:T(8,128)}) custom-call(f32[72]{0:T(128)} %hbm_wind_x.3, f32[72]{0:T(128)} %hbm_wind_y.3, f32[576,128]{1,0:T(8,128)} %collective-permute-done.hbm_before, f32[576,128]{1,0:T(8,128)} %collective-permute-done.1.hbm_after, f32[576,128]{1,0:T(8,128)} %get-tuple-element.8.hbm_tend), custom_call_target="tpu_custom_call" | custom-call | tf_op jit(solution)/shard_map/share/pallas_call | solution.py:496
  66.1 0.1 collective-permute-start.2
  66.1 1.6 %collective-permute-start.3 = (f32[8,128]{1,0:T(8,128)}, f32[8,128]{1,0:T(8,128)}, u32[]{:S(2)}, u32[]{:S(2)}) collective-permute-start(f32[8,128]{1,0:T(8,128)} %get-tuple-element.12), channel_id=1, source_target_pairs={{1,2},{3,0},{2,1},{0,3},{5,6},{7,4},{6,5},{4,7},{9,10},{11,8},{10,... | collective-permute-start | bytes 12296 | tf_op jit(solution)/shard_map/ppermute | solution.py:448
  67.7 2.2 %inner.1.hbm_inner = f32[576,128]{1,0:T(8,128)} custom-call(f32[576,128]{1,0:T(8,128)} %bitcast.8, f32[576,128]{1,0:T(8,128)} %get-tuple-element.9.hbm_shared, f32[2,58,8,128]{3,2,1,0:T(8,128)} %get-tuple-element.10.hbm_change), custom_call_target="tpu_custom_call" | custom-call | flops 1000000 | bytes 5000000 | tf_op jit(solution)/shard_map/inner/pallas_call | solution.py:521
  69.9 0.0 collective-permute-done.2.hbm_first
  69.9 0.0 collective-permute-done.3.hbm_second
  69.9 1.9 %outer.1 = f32[576,128]{1,0:T(8,128)} custom-call(f32[576,128]{1,0:T(8,128)} %inner.1.hbm_inner, f32[8,128]{1,0:T(8,128)} %collective-permute-done.2.hbm_first, f32[8,128]{1,0:T(8,128)} %collective-permute-done.3.hbm_second), custom_call_target="tpu_custom_call" | custom-call | tf_op jit(solution)/shard_map/outer/pallas_call | solution.py:538
Async XLA Ops:
  0.6 63.0 %collective-permute-start.1 = (f32[576,128]{1,0:T(8,128)}, f32[576,128]{1,0:T(8,128)}, u32[]{:S(2)}, u32[]{:S(2)}) collective-permute-start(f32[576,128]{1,0:T(8,128)} %bitcast.5), channel_id=1, source_target_pairs={{4,0},{8,4},{12,8},{0,12},{5,1},{9,5},{13,9},{1,13},{6,2},{10,6},{... | collective-permute-start | bytes 884744 | tf_op jit(solution)/shard_map/ppermute | solution.py:452
  5.7 57.9 %collective-permute-start = (f32[576,128]{1,0:T(8,128)}, f32[576,128]{1,0:T(8,128)}, u32[]{:S(2)}, u32[]{:S(2)}) collective-permute-start(f32[576,128]{1,0:T(8,128)} %bitcast.6), channel_id=1, source_target_pairs={{0,4},{4,8},{8,12},{12,0},{1,5},{5,9},{9,13},{13,1},{2,6},{6,10},{... | collective-permute-start | bytes 884744 | tf_op jit(solution)/shard_map/ppermute | solution.py:452
  66.1 3.9 %collective-permute-start.2 = (f32[8,128]{1,0:T(8,128)}, f32[8,128]{1,0:T(8,128)}, u32[]{:S(2)}, u32[]{:S(2)}) collective-permute-start(f32[8,128]{1,0:T(8,128)} %get-tuple-element.11), channel_id=1, source_target_pairs={{0,1},{2,3},{1,0},{3,2},{4,5},{6,7},{5,4},{7,6},{8,9},{10,11},{9,8... | collective-permute-start | bytes 12296 | tf_op jit(solution)/shard_map/ppermute | solution.py:448
  66.1 3.8 %collective-permute-start.3 = (f32[8,128]{1,0:T(8,128)}, f32[8,128]{1,0:T(8,128)}, u32[]{:S(2)}, u32[]{:S(2)}) collective-permute-start(f32[8,128]{1,0:T(8,128)} %get-tuple-element.12), channel_id=1, source_target_pairs={{1,2},{3,0},{2,1},{0,3},{5,6},{7,4},{6,5},{4,7},{9,10},{11,8},{10,... | collective-permute-start | bytes 12296 | tf_op jit(solution)/shard_map/ppermute | solution.py:448

commit v7 on v6

--- a/solution.py
+++ b/solution.py
@@ -189,12 +189,12 @@
 
 
 def outer_kernel(
-    hbm_inner, hbm_first, hbm_second, hbm_out, inner, met, sems, out_sem
+    hbm_inner, hbm_first, hbm_second, hbm_out, inner, met, halo, sems, out_sem
 ):
     copies = fetch(
         ((hbm_first, met.at[0]), (hbm_second, met.at[1]), (hbm_inner, inner)), sems
     )
-    for copy in copies:
+    for copy in copies[:2]:
         copy.wait()
     rows, lanes = inner.shape
     lane8 = lanes_of((8, lanes))
@@ -202,12 +202,13 @@
     at_left, at_right = met[1 - odd] * (0.5 * DT_DYN), met[odd] * (0.5 * DT_DYN)
     for v in range(rows // 8):
         at = slice(8 * v, 8 * v + 8)
-        halo = jnp.where(
+        halo[at, :] = jnp.where(
             lane8 == 0,
             pltpu.roll(at_left, (lanes - v) % lanes, 1),
             jnp.where(lane8 == lanes - 1, pltpu.roll(at_right, lanes - 1 - v, 1), 0.0),
         )
-        inner[at, :] = inner[at, :] + halo
+    copies[2].wait()
+    inner[...] = inner[...] + halo[...]
     copy = pltpu.make_async_copy(inner, hbm_out, out_sem)
     copy.start()
     copy.wait()
@@ -324,18 +325,18 @@
             other[k] = result[2 + side] - sat[k]
         return tuple(result)
 
-    carry = tuple(carry)
-    for c in range(PIECES):
-        for load in loads[c]:
-            load.wait()
-        carry = lax.fori_loop(cuts[c], cuts[c + 1], unpack, carry, unroll=4)
-
     for k in range(levels):
         for f in range(fields):
             keep = (1.0 - 2.0 * KAPPA - courant[k] - DT_CLOUD * relax[f, k]) * (1.0 / KAPPA)
             factors[f, k] = jnp.full((8, lanes), keep, jnp.float32)
         factors[fields, k] = jnp.full((8, lanes), courant[k] * (1.0 / KAPPA), jnp.float32)
         factors[fields + 1, k] = jnp.full((8, lanes), DT_CLOUD * cond_rate[k], jnp.float32)
+
+    carry = tuple(carry)
+    for c in range(PIECES):
+        for load in loads[c]:
+            load.wait()
+        carry = lax.fori_loop(cuts[c], cuts[c + 1], unpack, carry, unroll=4)
 
     def substep(src, dst, scale, inverse):
         for k in range(levels):
@@ -543,6 +544,7 @@
         scratch_shapes=[
             pltpu.VMEM((rows, lanes), f32),
             pltpu.VMEM((2, 8, lanes), f32),
+            pltpu.VMEM((rows, lanes), f32),
             dma((3,)),
             dma,
         ],

time: 72.1 us -> 71.7 us (level)
  no operation moved by 1% of the time
where the time goes in v7:
time: 71.7 us; the launch traced here: 71.5 us
  Pallas kernels  64 us (89%)
  starting transfers between devices  6.78 us (9%)
    pallas_call x1, Pallas kernels, body(): pl.pallas_call(cloud_kernel, out_shape=(pltpu.HBM(slots, jnp.bfloat16), p...  57.7 us
    ppermute x1, starting transfers between devices, body(): lax.ppermute(gcm, 'col', [(b, a) for a, b in ring])  5.1 us
    pallas_call x1, Pallas kernels, body(): pl.pallas_call(functools.partial(share_kernel, levels), out_shape=(pltpu....  2.41 us
    pallas_call x1, Pallas kernels, body(): pl.pallas_call(functools.partial(inner_kernel, levels, cloud_levels), out...  2.16 us
    pallas_call x1, Pallas kernels, body(): pl.pallas_call(outer_kernel, out_shape=pltpu.HBM((rows, lanes), f32), in_...  1.74 us
    ppermute x2, starting transfers between devices, swapped(): return lax.ppermute(cells, axis, pairs + [(b, a) for a, b in pairs])  1.68 us
  transfers between devices with their start and end apart: 4, of which 0 were waited for; matrix products, arithmetic and copies ran while one was open for 0% of the time, Pallas kernels for 84%

profile of v7, /device:TPU:0, one launch (start us, length us, event | category | flops | bytes accessed | tf_op | source)
XLA Modules:
  0.0 71.5 jit_solution(8724456503538662533)
XLA Ops:
  0.6 5.1 %collective-permute-start.1 = (f32[576,128]{1,0:T(8,128)}, f32[576,128]{1,0:T(8,128)}, u32[]{:S(2)}, u32[]{:S(2)}) collective-permute-start(f32[576,128]{1,0:T(8,128)} %bitcast.5), channel_id=1, source_target_pairs={{4,0},{8,4},{12,8},{0,12},{5,1},{9,5},{13,9},{1,13},{6,2},{10,6},{... | collective-permute-start | bytes 884744 | tf_op jit(solution)/shard_map/ppermute | solution.py:453
  5.7 0.0 collective-permute-start
  5.7 57.7 %cloud.1 = (bf16[2,58,128,128]{3,2,1,0:T(8,128)(2,1)}, f32[2,58,8,128]{3,2,1,0:T(8,128)}, f32[576,128]{1,0:T(8,128)}) custom-call(f32[58]{0:T(128)} %hbm_courant.1, f32[2,58]{1,0:T(2,128)} %hbm_relax.1, f32[58]{0:T(128)} %hbm_sat.1, f32[58]{0:T(128)} %hbm_cond.1, f32[576,128]{1,0:T(8,128)} %bitcast.7, s32[4,128]{1,0:T(4,128)} %hbm_active.1, f32[72]{0:T(128)} %hbm_wind_x.3, ...), custom_call_target="tpu_custom_call" | custom-call | flops 60000000 | bytes 200000000 | tf_op jit(solution)/shard_map/cloud/pallas_call | solution.py:457
  63.5 0.0 collective-permute-done.1.hbm_after
  63.5 0.0 collective-permute-done.hbm_before
  63.5 2.4 %share.1 = (f32[576,128]{1,0:T(8,128)}, f32[8,128]{1,0:T(8,128)}, f32[8,128]{1,0:T(8,128)}) custom-call(f32[72]{0:T(128)} %hbm_wind_x.3, f32[72]{0:T(128)} %hbm_wind_y.3, f32[576,128]{1,0:T(8,128)} %collective-permute-done.hbm_before, f32[576,128]{1,0:T(8,128)} %collective-permute-done.1.hbm_after, f32[576,128]{1,0:T(8,128)} %get-tuple-element.8.hbm_tend), custom_call_target="tpu_custom_call" | custom-call | tf_op jit(solution)/shard_map/share/pallas_call | solution.py:497
  65.9 0.1 collective-permute-start.2
  66.0 1.6 %collective-permute-start.3 = (f32[8,128]{1,0:T(8,128)}, f32[8,128]{1,0:T(8,128)}, u32[]{:S(2)}, u32[]{:S(2)}) collective-permute-start(f32[8,128]{1,0:T(8,128)} %get-tuple-element.12), channel_id=1, source_target_pairs={{1,2},{3,0},{2,1},{0,3},{5,6},{7,4},{6,5},{4,7},{9,10},{11,8},{10,... | collective-permute-start | bytes 12296 | tf_op jit(solution)/shard_map/ppermute | solution.py:449
  67.6 2.2 %inner.1.hbm_inner = f32[576,128]{1,0:T(8,128)} custom-call(f32[576,128]{1,0:T(8,128)} %bitcast.8, f32[576,128]{1,0:T(8,128)} %get-tuple-element.9.hbm_shared, f32[2,58,8,128]{3,2,1,0:T(8,128)} %get-tuple-element.10.hbm_change), custom_call_target="tpu_custom_call" | custom-call | flops 1000000 | bytes 5000000 | tf_op jit(solution)/shard_map/inner/pallas_call | solution.py:522
  69.8 0.0 collective-permute-done.2.hbm_first
  69.8 0.0 collective-permute-done.3.hbm_second
  69.8 1.7 %outer.1 = f32[576,128]{1,0:T(8,128)} custom-call(f32[576,128]{1,0:T(8,128)} %inner.1.hbm_inner, f32[8,128]{1,0:T(8,128)} %collective-permute-done.2.hbm_first, f32[8,128]{1,0:T(8,128)} %collective-permute-done.3.hbm_second), custom_call_target="tpu_custom_call" | custom-call | tf_op jit(solution)/shard_map/outer/pallas_call | solution.py:539
Async XLA Ops:
  0.6 62.8 %collective-permute-start.1 = (f32[576,128]{1,0:T(8,128)}, f32[576,128]{1,0:T(8,128)}, u32[]{:S(2)}, u32[]{:S(2)}) collective-permute-start(f32[576,128]{1,0:T(8,128)} %bitcast.5), channel_id=1, source_target_pairs={{4,0},{8,4},{12,8},{0,12},{5,1},{9,5},{13,9},{1,13},{6,2},{10,6},{... | collective-permute-start | bytes 884744 | tf_op jit(solution)/shard_map/ppermute | solution.py:453
  5.7 57.8 %collective-permute-start = (f32[576,128]{1,0:T(8,128)}, f32[576,128]{1,0:T(8,128)}, u32[]{:S(2)}, u32[]{:S(2)}) collective-permute-start(f32[576,128]{1,0:T(8,128)} %bitcast.6), channel_id=1, source_target_pairs={{0,4},{4,8},{8,12},{12,0},{1,5},{5,9},{9,13},{13,1},{2,6},{6,10},{... | collective-permute-start | bytes 884744 | tf_op jit(solution)/shard_map/ppermute | solution.py:453
  65.9 3.9 %collective-permute-start.2 = (f32[8,128]{1,0:T(8,128)}, f32[8,128]{1,0:T(8,128)}, u32[]{:S(2)}, u32[]{:S(2)}) collective-permute-start(f32[8,128]{1,0:T(8,128)} %get-tuple-element.11), channel_id=1, source_target_pairs={{0,1},{2,3},{1,0},{3,2},{4,5},{6,7},{5,4},{7,6},{8,9},{10,11},{9,8... | collective-permute-start | bytes 12296 | tf_op jit(solution)/shard_map/ppermute | solution.py:449
  66.0 3.8 %collective-permute-start.3 = (f32[8,128]{1,0:T(8,128)}, f32[8,128]{1,0:T(8,128)}, u32[]{:S(2)}, u32[]{:S(2)}) collective-permute-start(f32[8,128]{1,0:T(8,128)} %get-tuple-element.12), channel_id=1, source_target_pairs={{1,2},{3,0},{2,1},{0,3},{5,6},{7,4},{6,5},{4,7},{9,10},{11,8},{10,... | collective-permute-start | bytes 12296 | tf_op jit(solution)/shard_map/ppermute | solution.py:449
